TPU v7x, 512 devices: a whole 4x4x16 slice. The times are simulated.
512 devices in a mesh: rep: 8 (over x, y_lo), exp: 64 (over z, y_hi, core).
Axes of the slice: x: 4, y: 4 (y_hi: 2, y_lo: 2; y = y_hi * 2 + y_lo), z: 16, core: 2. Of those that a mesh axis runs over, the one named last changes fastest.
Arguments:
- hidden_in: bfloat16 [8192, 2048], P('exp', 'rep'), may hold values from -36 to 36
- norm_gain: float32 [2048], replicated, may hold values from 0.25 to 1.75
- route_ids: int32 [8192, 2], P('exp'), may hold values from 0 to 63, all different within a row; in each aligned block of 128 rows (0 to 127, 128 to 255, ...) at most 5 rows name the same one
- route_weights: float32 [8192, 2], P('exp'), may hold values from 0.05 to 0.6
- w_gate: bfloat16 [64, 1536, 2048], P('exp', 'rep'), may hold values from -0.125 to 0.125
- w_up: bfloat16 [64, 1536, 2048], P('exp', 'rep'), may hold values from -0.125 to 0.125
- w_down: bfloat16 [64, 1536, 2048], P('exp', 'rep'), may hold values from -0.15625 to 0.15625
- out_grad: bfloat16 [8192, 2048], P('exp', 'rep'), may hold values from -6 to 6
Outputs:
- layer_out: bfloat16 [8192, 2048], P(('exp', 'rep'))
- input_grad: bfloat16 [8192, 2048], P(('exp', 'rep'))
- route_grad: float32 [8192, 2], P(('exp', 'rep'))
- gate_update: bfloat16 [64, 1536, 2048], P('exp', 'rep')
- up_update: bfloat16 [64, 1536, 2048], P('exp', 'rep')
- down_update: bfloat16 [64, 1536, 2048], P('exp', 'rep')
Inputs may be any that keep to these rules, and one draw needn't show every extreme that they name: `route_ids`: each row names 2 different experts. Within each aligned block of 128 rows (the tokens of one index of exp) no expert is named by more than 5 rows, and in every draw some expert is named by exactly 5 rows of some block.
All inputs are finite; a program needn't handle non-finite values.
Results may differ from a plain program's by a relative error of at most 0.02.
Values may be sent and summed in bfloat16 or wider, within the bound.
A program may use at most 64 MiB of HBM per device.

v0:
```python
import jax
import jax.numpy as jnp
from jax import lax
from jax.sharding import PartitionSpec as P

epsilon = 1e-06


def route_table(route_ids, expert_count, capacity):
    token_count, fanout = route_ids.shape
    expert_range = jnp.arange(expert_count, dtype=jnp.int32)
    per_expert = jnp.sum(
        (route_ids[:, :, None] == expert_range[None, None, :]).astype(jnp.int32), axis=1
    )
    earlier = jnp.cumsum(per_expert, axis=0) - per_expert
    slot_index = jnp.take_along_axis(earlier, route_ids, axis=1)
    position = route_ids * capacity + slot_index
    source_route = (
        jnp.full((expert_count * capacity,), -1, jnp.int32)
        .at[position.reshape(-1)]
        .set(jnp.arange(token_count * fanout, dtype=jnp.int32))
    )
    return (position, source_route)


def fill_rows(source_route, fanout, normed, gradient, route_weights):
    filled = source_route >= 0
    route_safe = jnp.maximum(source_route, 0)
    token_safe = route_safe // fanout
    weight_rows = jnp.where(
        filled, route_weights.reshape(-1)[route_safe], jnp.zeros((), jnp.float32)
    )
    normed_rows = jnp.where(filled[:, None], normed[token_safe], jnp.zeros((), jnp.bfloat16))
    grad_rows = (weight_rows[:, None] * gradient[token_safe].astype(jnp.float32)).astype(
        jnp.bfloat16
    )
    return (normed_rows, grad_rows)


def body(hidden_in, norm_gain, route_ids, route_weights, w_gate, w_up, w_down, out_grad):
    rep_count = lax.axis_size("rep")
    expert_count = lax.axis_size("exp")
    rep_position = lax.axis_index("rep")
    token_count, fanout = route_ids.shape
    capacity = 5 * token_count * fanout // (4 * expert_count)
    row_count = token_count // rep_count
    full_in, full_grad = (
        lax.all_gather(hidden_in, "rep", axis=1, tiled=True),
        lax.all_gather(out_grad, "rep", axis=1, tiled=True),
    )
    feature_count = full_in.shape[1]
    inputs_f32 = full_in.astype(jnp.float32)
    root_mean = jnp.sqrt(jnp.mean(inputs_f32 * inputs_f32, axis=1, keepdims=True) + epsilon)
    normed = (inputs_f32 * norm_gain[None, :] / root_mean).astype(jnp.bfloat16)
    position, source_route = route_table(route_ids, expert_count, capacity)
    send_normed, send_grad = fill_rows(source_route, fanout, normed, full_grad, route_weights)
    got_normed, got_grad = (
        lax.all_to_all(send_normed, "exp", split_axis=0, concat_axis=0, tiled=True),
        lax.all_to_all(send_grad, "exp", split_axis=0, concat_axis=0, tiled=True),
    )
    rows_normed, rows_grad = (got_normed, got_grad)
    gate_matrix = w_gate[0]
    up_matrix = w_up[0]
    down_matrix = w_down[0]
    contract_last = (((1,), (1,)), ((), ()))
    gate_pre = lax.dot_general(
        rows_normed, gate_matrix, contract_last, preferred_element_type=jnp.float32
    )
    up_pre = lax.dot_general(
        rows_normed, up_matrix, contract_last, preferred_element_type=jnp.float32
    )
    sigmoid_gate = jax.nn.sigmoid(gate_pre)
    activated = gate_pre * sigmoid_gate
    hidden = (activated * up_pre).astype(jnp.bfloat16)
    out_part = jnp.dot(hidden, down_matrix, preferred_element_type=jnp.float32).astype(jnp.bfloat16)
    hidden_grad = lax.dot_general(
        rows_grad, down_matrix, contract_last, preferred_element_type=jnp.float32
    )
    gate_grad = (
        hidden_grad * up_pre * sigmoid_gate * (1.0 + gate_pre * (1.0 - sigmoid_gate))
    ).astype(jnp.bfloat16)
    up_grad = (hidden_grad * activated).astype(jnp.bfloat16)
    input_part = jnp.dot(gate_grad, gate_matrix, preferred_element_type=jnp.float32)
    input_part = (
        input_part + jnp.dot(up_grad, up_matrix, preferred_element_type=jnp.float32)
    ).astype(jnp.bfloat16)
    back_out, back_input = (
        lax.all_to_all(out_part, "exp", split_axis=0, concat_axis=0, tiled=True),
        lax.all_to_all(input_part, "exp", split_axis=0, concat_axis=0, tiled=True),
    )
    contract_rows = (((0,), (0,)), ((), ()))
    down_update = lax.dot_general(
        hidden, rows_grad, contract_rows, preferred_element_type=jnp.float32
    ).astype(jnp.bfloat16)
    gate_update = lax.dot_general(
        gate_grad, rows_normed, contract_rows, preferred_element_type=jnp.float32
    ).astype(jnp.bfloat16)
    up_update = lax.dot_general(
        up_grad, rows_normed, contract_rows, preferred_element_type=jnp.float32
    ).astype(jnp.bfloat16)
    picked_out = back_out[position].astype(jnp.float32)
    picked_input = back_input[position].astype(jnp.float32)
    combined_out = jnp.sum(route_weights[:, :, None] * picked_out, axis=1)
    combined_input = jnp.sum(picked_input, axis=1)
    route_dots = jnp.sum(picked_out * full_grad.astype(jnp.float32)[:, None, :], axis=2)
    share_out, share_input, share_dots = (
        lax.psum_scatter(
            combined_out.astype(jnp.bfloat16), "rep", scatter_dimension=0, tiled=True
        ).astype(jnp.float32),
        lax.psum_scatter(
            combined_input.astype(jnp.bfloat16), "rep", scatter_dimension=0, tiled=True
        ).astype(jnp.float32),
        lax.psum_scatter(
            route_dots.astype(jnp.bfloat16), "rep", scatter_dimension=0, tiled=True
        ).astype(jnp.float32),
    )
    row_start = rep_position * row_count
    own_inputs = lax.dynamic_slice_in_dim(inputs_f32, row_start, row_count, 0)
    own_root = lax.dynamic_slice_in_dim(root_mean, row_start, row_count, 0)
    layer_out = (own_inputs + share_out).astype(jnp.bfloat16)
    scaled = norm_gain[None, :] * share_input
    inner = jnp.sum(scaled * own_inputs, axis=1, keepdims=True)
    input_grad = (scaled / own_root - own_inputs * inner / (feature_count * own_root**3)).astype(
        jnp.bfloat16
    )
    return (
        layer_out,
        input_grad,
        share_dots,
        gate_update[None],
        up_update[None],
        down_update[None],
    )


def solution(mesh):
    placed = (
        P("exp", "rep"),
        P(),
        P("exp", None),
        P("exp", None),
        P("exp", "rep", None),
        P("exp", "rep", None),
        P("exp", "rep", None),
        P("exp", "rep"),
    )
    return jax.shard_map(
        body,
        mesh=mesh,
        in_specs=placed,
        out_specs=(
            P(("exp", "rep"), None),
            P(("exp", "rep"), None),
            P(("exp", "rep"), None),
            P("exp", "rep", None),
            P("exp", "rep", None),
            P("exp", "rep", None),
        ),
        check_vma=False,
    )
```

profile of v0, /device:TPU:1, one launch (start us, length us, event | category | flops | bytes accessed | tf_op | source)
XLA Modules:
  0.0 605.1 jit_solution(7125476847058957025)
XLA Ops:
  9.2 1.9 gather_fusion.5
  13.7 23.4 %all_gather.6 = bf16[128,2048]{1,0:T(8,128)(2,1)S(1)} all-gather(bf16[128,256]{1,0:T(8,128)(2,1)S(1)} %copy-done.18), channel_id=1, replica_groups=mesh['rep'=8,'exp'=64] {'rep'}, dimensions={1}, use_global_device_ids=true | all-gather | bytes 589824 | tf_op jit(solution)/shard_map/all_gather | solution.py:48
  38.0 3.0 gather_fusion
  41.1 2.4 gather.23
  43.7 2.5 gather_fusion.2
  48.0 25.8 %all-to-all-start = ((bf16[64,5,2048]{2,1,0:T(8,128)(2,1)}), bf16[64,5,2048]{2,1,0:T(8,128)(2,1)}, u32[]{:S(2)}, u32[]{:S(2)}) async-start(bf16[64,5,2048]{2,1,0:T(8,128)(2,1)} %broadcast_select_fusion), calls=%async_computation | async-start | bytes 4194304 | tf_op jit(solution)/shard_map/all_to_all | solution.py:58
  73.9 24.9 %all_gather.7 = bf16[128,2048]{1,0:T(8,128)(2,1)S(1)} all-gather(bf16[128,256]{1,0:T(8,128)(2,1)S(1)} %copy-done.19), channel_id=1, replica_groups=mesh['rep'=8,'exp'=64] {'rep'}, dimensions={1}, use_global_device_ids=true | all-gather | bytes 589824 | tf_op jit(solution)/shard_map/all_gather | solution.py:49
  98.8 2.4 gather_fusion.3
  101.3 2.2 reshape.110
  103.4 3.9 multiply_convert_fusion
  107.3 64.7 %all-to-all-done = bf16[64,5,2048]{2,1,0:T(8,128)(2,1)} async-done(((bf16[64,5,2048]{2,1,0:T(8,128)(2,1)}), bf16[64,5,2048]{2,1,0:T(8,128)(2,1)}, u32[]{:S(2)}, u32[]{:S(2)}) %all-to-all-start) | async-done | bytes 1310752 | tf_op jit(solution)/shard_map/all_to_all | solution.py:58
  172.0 8.2 %all-to-all-start.2 = ((bf16[64,5,2048]{2,1,0:T(8,128)(2,1)}), bf16[64,5,2048]{2,1,0:T(8,128)(2,1)}, u32[]{:S(2)}, u32[]{:S(2)}) async-start(bf16[64,5,2048]{2,1,0:T(8,128)(2,1)} %multiply_convert_fusion), calls=%async_computation.3 | async-start | bytes 4194304 | tf_op jit(solution)/shard_map/all_to_all | solution.py:59
  180.3 2.6 all_to_all.29
  185.7 92.8 %all-to-all-done.2 = bf16[64,5,2048]{2,1,0:T(8,128)(2,1)} async-done(((bf16[64,5,2048]{2,1,0:T(8,128)(2,1)}), bf16[64,5,2048]{2,1,0:T(8,128)(2,1)}, u32[]{:S(2)}, u32[]{:S(2)}) %all-to-all-start.2) | async-done | bytes 1310752 | tf_op jit(solution)/shard_map/all_to_all | solution.py:59
  278.6 3.6 all_to_all.34
  282.2 2.8 multiply_convert_fusion.1
  287.3 3.4 all_to_all.30
  290.7 8.3 %all-to-all-start.1 = ((bf16[64,5,2048]{2,1,0:T(8,128)(2,1)}), bf16[64,5,2048]{2,1,0:T(8,128)(2,1)}, u32[]{:S(2)}, u32[]{:S(2)}) async-start(bf16[64,5,2048]{2,1,0:T(8,128)(2,1)} %all_to_all.30), calls=%async_computation.1 | async-start | bytes 4194304 | tf_op jit(solution)/shard_map/all_to_all | solution.py:88
  301.8 3.4 all_to_all.35
  305.2 92.5 %all-to-all-done.1 = bf16[64,5,2048]{2,1,0:T(8,128)(2,1)} async-done(((bf16[64,5,2048]{2,1,0:T(8,128)(2,1)}), bf16[64,5,2048]{2,1,0:T(8,128)(2,1)}, u32[]{:S(2)}, u32[]{:S(2)}) %all-to-all-start.1) | async-done | bytes 1310752 | tf_op jit(solution)/shard_map/all_to_all | solution.py:88
  397.7 7.8 %all-to-all-start.3 = ((bf16[64,5,2048]{2,1,0:T(8,128)(2,1)}), bf16[64,5,2048]{2,1,0:T(8,128)(2,1)}, u32[]{:S(2)}, u32[]{:S(2)}) async-start(bf16[64,5,2048]{2,1,0:T(8,128)(2,1)} %all_to_all.35), calls=%async_computation.4 | async-start | bytes 4194304 | tf_op jit(solution)/shard_map/all_to_all | solution.py:89
  406.9 2.6 all_to_all.32
  409.5 2.4 gather_fusion.1
  411.9 3.5 reshape.172
  415.4 6.1 %multiply_reduce_fusion = (bf16[128,2]{1,0:T(8,128)(2,1)}, bf16[128,2048]{1,0:T(8,128)(2,1)}) fusion(f32[128,2,2048]{2,1,0:T(2,128)} %reshape.172, f32[128,2048]{1,0:T(8,128)S(1)} %copy-done.4, f32[128,2]{1,0:T(8,128)S(1)} %copy-done.11), kind=kLoop, calls=%fused_computation.17 | loop fusion | flops 1834752 | bytes 3671552 | tf_op jit(solution)/shard_map/reduce_sum | solution.py:105
  421.8 82.0 %all-to-all-done.3 = bf16[64,5,2048]{2,1,0:T(8,128)(2,1)} async-done(((bf16[64,5,2048]{2,1,0:T(8,128)(2,1)}), bf16[64,5,2048]{2,1,0:T(8,128)(2,1)}, u32[]{:S(2)}, u32[]{:S(2)}) %all-to-all-start.3) | async-done | bytes 1310752 | tf_op jit(solution)/shard_map/all_to_all | solution.py:89
  503.8 2.6 all_to_all.37
  506.4 2.4 gather_fusion.4
  508.7 2.5 reshape.148
  511.3 4.6 reduce_sum.60
  523.6 26.4 %reduce-scatter.8.cloned.1.call-done = bf16[16,2048]{1,0:T(8,128)(2,1)} async-done(((bf16[128,2048]{1,0:T(8,128)(2,1)}), bf16[16,2048]{1,0:T(8,128)(2,1)}) %reduce-scatter.8.cloned.1.call-update) | async-done | bytes 65552 | tf_op jit(solution)/shard_map/reduce_scatter | solution.py:110
  551.1 45.8 %reduce-scatter.6.cloned.1.call-done = bf16[16,2048]{1,0:T(8,128)(2,1)} async-done(((bf16[128,2048]{1,0:T(8,128)(2,1)}), bf16[16,2048]{1,0:T(8,128)(2,1)}) %reduce-scatter.6.cloned.1.call-update) | async-done | bytes 65552 | tf_op jit(solution)/shard_map/reduce_scatter | solution.py:107
  (102 shorter events, 27.4 us)
Async XLA Ops:
  7.2 275.0 %copy-start = (bf16[1,192,2048]{2,1,0:T(8,128)(2,1)S(1)}, bf16[1,192,2048]{2,1,0:T(8,128)(2,1)}, u32[]{:S(2)}) copy-start(bf16[1,192,2048]{2,1,0:T(8,128)(2,1)} %param.14) | copy-start | bytes 2359300
  9.2 2.2 copy-start.20
  9.2 4.5 copy-start.18
  11.2 26.7 %copy-start.16 = (f32[2048]{0:T(1024)S(1)}, f32[2048]{0:T(1024)}, u32[]{:S(2)}) copy-start(f32[2048]{0:T(1024)} %param.9) | copy-start | bytes 24580
  37.1 0.8 copy-start.1
  37.9 3.2 copy-start.22
  41.1 2.4 copy-start.24
  43.6 4.4 copy-start.10
  48.0 25.9 %copy-start.19 = (bf16[128,256]{1,0:T(8,128)(2,1)S(1)}, bf16[128,256]{1,0:T(8,128)(2,1)}, u32[]{:S(2)}) copy-start(bf16[128,256]{1,0:T(8,128)(2,1)} %param.15) | copy-start | bytes 196612
  48.0 124.1 %all-to-all-start = ((bf16[64,5,2048]{2,1,0:T(8,128)(2,1)}), bf16[64,5,2048]{2,1,0:T(8,128)(2,1)}, u32[]{:S(2)}, u32[]{:S(2)}) async-start(bf16[64,5,2048]{2,1,0:T(8,128)(2,1)} %broadcast_select_fusion), calls=%async_computation | async-start | bytes 4194304 | tf_op jit(solution)/shard_map/all_to_all | solution.py:58
  172.0 106.6 %all-to-all-start.2 = ((bf16[64,5,2048]{2,1,0:T(8,128)(2,1)}), bf16[64,5,2048]{2,1,0:T(8,128)(2,1)}, u32[]{:S(2)}, u32[]{:S(2)}) async-start(bf16[64,5,2048]{2,1,0:T(8,128)(2,1)} %multiply_convert_fusion), calls=%async_computation.3 | async-start | bytes 4194304 | tf_op jit(solution)/shard_map/all_to_all | solution.py:59
  180.3 2.7 copy-start.5
  182.9 1.4 copy-start.6
  285.0 0.7 copy-start.12
  285.0 14.0 %copy-start.8 = (bf16[320,192]{0,1:T(8,128)(2,1)}, bf16[320,192]{0,1:T(8,128)(2,1)S(1)}, u32[]{:S(2)}) copy-start(bf16[320,192]{0,1:T(8,128)(2,1)S(1)} %get-tuple-element.17) | copy-start | bytes 368644
  290.7 107.0 %all-to-all-start.1 = ((bf16[64,5,2048]{2,1,0:T(8,128)(2,1)}), bf16[64,5,2048]{2,1,0:T(8,128)(2,1)}, u32[]{:S(2)}, u32[]{:S(2)}) async-start(bf16[64,5,2048]{2,1,0:T(8,128)(2,1)} %all_to_all.30), calls=%async_computation.1 | async-start | bytes 4194304 | tf_op jit(solution)/shard_map/all_to_all | solution.py:88
  299.1 1.1 copy-start.7
  299.1 1.1 copy-start.14
  397.7 106.1 %all-to-all-start.3 = ((bf16[64,5,2048]{2,1,0:T(8,128)(2,1)}), bf16[64,5,2048]{2,1,0:T(8,128)(2,1)}, u32[]{:S(2)}, u32[]{:S(2)}) async-start(bf16[64,5,2048]{2,1,0:T(8,128)(2,1)} %all_to_all.35), calls=%async_computation.4 | async-start | bytes 4194304 | tf_op jit(solution)/shard_map/all_to_all | solution.py:89
  405.5 1.2 copy-start.21
  405.5 116.7 %reduce-scatter.10.cloned.1.call-start = ((), (), s32[]{:S(2)}) async-start(), calls=%async_computation.9 | async-start | bytes 36864
  411.9 3.5 copy-start.4
  411.9 3.5 copy-start.11
  421.5 128.5 %reduce-scatter.8.cloned.1.call-start = ((), (), s32[]{:S(2)}) async-start(), calls=%async_computation.8 | async-start | bytes 589824 | tf_op jit(solution)/shard_map/reduce_scatter | solution.py:110
  511.3 5.4 copy-start.2
  515.9 1.9 copy-start.23
  515.9 1.9 copy-start.9
  515.9 81.0 %reduce-scatter.6.cloned.1.call-start = ((), (), s32[]{:S(2)}) async-start(), calls=%async_computation.7 | async-start | bytes 589824 | tf_op jit(solution)/shard_map/reduce_scatter | solution.py:107
  517.8 1.5 copy-start.15
  519.3 1.5 copy-start.3
  519.3 1.5 copy-start.13
  520.8 29.2 %copy-start.17 = (f32[2048]{0:T(1024)S(1)}, f32[2048]{0:T(1024)}, u32[]{:S(2)}) copy-start(f32[2048]{0:T(1024)} %param.9) | copy-start | bytes 24580
Sparse Core Ops, SparseCore 0:
  421.7 41.2 reduce-scatter.9
  516.0 33.9 reduce-scatter.7
  552.8 44.0 reduce-scatter.5
where the time goes:
time: 610 us; the launch traced here: 605 us
  waiting for transfers between devices  405 us (66%)
  starting transfers between devices  50.5 us (8%)
  local copies, waits for them, and re-layouts  49 us (8%)
  blocking collectives  48.3 us (8%)
  other arithmetic  24.4 us (4%)
  between operations  14.1 us (2%)
  matrix products  13.7 us (2%)
    all_to_all x1, waiting for transfers between devices, body(): lax.all_to_all(send_grad, 'exp', split_axis=0, concat_axis=0, tiled=True)  92.8 us
    all_to_all x1, waiting for transfers between devices, body(): lax.all_to_all(out_part, 'exp', split_axis=0, concat_axis=0, tiled=True)  92.5 us
    all_to_all x1, waiting for transfers between devices, body(): lax.all_to_all(input_part, 'exp', split_axis=0, concat_axis=0, tiled=True)  82 us
    all_to_all x1, waiting for transfers between devices, body(): lax.all_to_all(send_normed, 'exp', split_axis=0, concat_axis=0, tiled=True)  64.7 us
    reduce_scatter x1, waiting for transfers between devices, body(): lax.psum_scatter(combined_out.astype(jnp.bfloat16), 'rep', scatter_dimens...  45.8 us
    reduce_scatter x1, waiting for transfers between devices, body(): lax.psum_scatter(combined_input.astype(jnp.bfloat16), 'rep', scatter_dime...  26.4 us
    all_to_all x1, starting transfers between devices, body(): lax.all_to_all(send_normed, 'exp', split_axis=0, concat_axis=0, tiled=True)  25.8 us
    all_gather x1, blocking collectives, body(): lax.all_gather(out_grad, 'rep', axis=1, tiled=True)  24.9 us
  transfers between devices with their start and end apart: 7, of which 6 were waited for; matrix products, arithmetic and copies ran while one was open for 7% of the time, Pallas kernels for 0%

commit v1 on v0

v1 whole, which is shorter than its diff:
```python
import functools

import jax
import jax.numpy as jnp
from jax import lax
from jax.experimental import pallas as pl
from jax.experimental.pallas import tpu as pltpu
from jax.sharding import PartitionSpec as P

MESH = pl.DeviceIdType.MESH
EPSILON = 1e-06
NZ = 16
NJ = 4
WIDTH = 256
CHUNKS = 5
ROWS = 64
F32 = jnp.float32
BF16 = jnp.bfloat16


def z_offset(c, m):
    if m == 0:
        return c + 1
    if m == 1:
        return 15 - c
    if m == 2:
        return 8 - c
    return jnp.where(c == 0, 0, 8 + c)


def offset_rows(place):
    c, m = place >> 2, place & 3
    far = jnp.where(c == 0, 0, 8 + c)
    return jnp.where(m == 0, c + 1, jnp.where(m == 1, 15 - c, jnp.where(m == 2, 8 - c, far)))


def iota(shape, dim):
    return lax.broadcasted_iota(jnp.int32, shape, dim)


def dot(a, b, dims):
    return lax.dot_general(a, b, ((dims[:1], dims[1:]), ((), ())), preferred_element_type=F32)


def kernel(
    h_ref, g_ref, ids_ref, wrow_ref, wcol_ref, gain_ref, wg_hbm, wu_hbm, wd_hbm,
    lo_ref, ig_ref, rg_ref, gu_hbm, uu_hbm, du_hbm,
    wg, wu, wd, gu, uu, du,
    tokh, tokg, meta, hx, zmain, zleft, leftin, gat, nrm, par, got, fmain, fleft,
    fmain_in, fleft_in, loc, loc_in, fin, fin_in, hid, ggr, ugr, ht, ggt, ugt,
    w_sem, o_sem, tok_send, tok_recv, hx_send, hx_recv, zm_send, zm_recv, zl_send, zl_recv,
    c_send, c_recv, e_send, e_recv, fm_send, fm_recv, fl_send, fl_recv, l_send, l_recv, y_send, y_recv,
):
    reps = lax.axis_size("rep")
    features = reps * WIDTH
    share = h_ref.shape[0] // reps
    rep = lax.axis_index("rep")
    exp = lax.axis_index("exp")
    z, j = exp // NJ, exp % NJ

    def at_z(off):
        return {"exp": lax.rem(z + off, NZ) * NJ + j}

    def at_j(d):
        return {"exp": z * NJ + lax.rem(j + d, NJ)}

    def at_j_back(d):
        return {"exp": z * NJ + lax.rem(j + NJ - d, NJ)}

    def at_rep(ro):
        return {"rep": lax.rem(rep + ro, reps)}

    def send(src, dst, ssem, rsem, device):
        pltpu.make_async_remote_copy(
            src_ref=src, dst_ref=dst, send_sem=ssem, recv_sem=rsem, device_id=device, device_id_type=MESH
        ).start()

    def wait(ref, sem):
        pltpu.make_async_copy(ref, ref, sem).wait()

    weights = [
        pltpu.make_async_copy(wg_hbm, wg, w_sem.at[0]),
        pltpu.make_async_copy(wu_hbm, wu, w_sem.at[1]),
        pltpu.make_async_copy(wd_hbm, wd, w_sem.at[2]),
    ]
    for copy in weights:
        copy.start()

    barrier = pltpu.get_barrier_semaphore()

    def greet(off, carry):
        pl.semaphore_signal(barrier, inc=1, device_id=at_z(off), device_id_type=MESH)
        return carry

    lax.fori_loop(1, NZ, greet, 0)
    for d in range(1, NJ):
        pl.semaphore_signal(barrier, inc=1, device_id=at_j(d), device_id_type=MESH)
    for ro in range(1, reps):
        pl.semaphore_signal(barrier, inc=1, device_id=at_rep(ro), device_id_type=MESH)

    ids = ids_ref[...]
    expert_rows = iota((NZ * NJ, 128), 0)
    hits = [(expert_rows == ids[k : k + 1, :]).astype(F32) for k in range(2)]
    before = (iota((128, 128), 0) < iota((128, 128), 1)).astype(F32).astype(BF16)
    earlier = dot((hits[0] + hits[1]).astype(BF16), before, (1, 0))
    for k in range(2):
        number = jnp.sum(hits[k] * earlier, axis=0, keepdims=True)
        meta[0, k : k + 1, :] = ids[k : k + 1, :].astype(F32) * 8.0 + number
    meta[0, 2:4, :] = wrow_ref[...]

    pl.semaphore_wait(barrier, NZ - 1 + NJ - 1 + reps - 1)

    for d in range(1, NJ):
        send(meta.at[0], meta.at[d], tok_send.at[0], tok_recv.at[0, d], at_j(d))
        send(h_ref, tokh.at[d], tok_send.at[1], tok_recv.at[1, d], at_j(d))
        send(g_ref, tokg.at[d], tok_send.at[2], tok_recv.at[2, d], at_j(d))
    own_rows = pl.ds(pl.multiple_of(rep * share, 16), share)
    for ro in range(1, reps):
        to = pl.multiple_of(lax.rem(rep + ro, reps) * share, 16)
        send(h_ref.at[pl.ds(to, share), :], hx.at[rep], hx_send, hx_recv, at_rep(ro))
    hx[rep] = h_ref[own_rows, :]
    tokh[0] = h_ref[...]
    tokg[0] = g_ref[...]
    for d in range(1, NJ):
        wait(meta.at[d], tok_recv.at[0, d])
        wait(tokh.at[d], tok_recv.at[1, d])
        wait(tokg.at[d], tok_recv.at[2, d])

    def pick(code, block):
        rows_h = rows_g = weight = None
        for d in range(NJ):
            mine = jnp.where(block == d, code, -1.0)
            one = [mine == meta[d, k : k + 1, :] for k in range(2)]
            both = (one[0] | one[1]).astype(F32).astype(BF16)
            w = jnp.sum(
                jnp.where(one[0], meta[d, 2:3, :], 0.0) + jnp.where(one[1], meta[d, 3:4, :], 0.0), axis=1, keepdims=True
            )
            h, g = dot(both, tokh[d], (1, 0)), dot(both, tokg[d], (1, 0))
            rows_h = h if d == 0 else rows_h + h
            rows_g = g if d == 0 else rows_g + g
            weight = w if d == 0 else weight + w
        return rows_h.astype(BF16), (weight * rows_g).astype(BF16)

    def code_of(place, number):
        plane = (z + offset_rows(place)) & (NZ - 1)
        return ((plane * NJ + j) * 8 + number).astype(F32)

    for c in range(4):
        r = iota((ROWS, 1), 0)
        rows_h, rows_g = pick(code_of(4 * c + (r >> 4), r & 3), (r >> 2) & 3)
        zmain[c * ROWS : (c + 1) * ROWS, 0:WIDTH] = rows_h
        zmain[c * ROWS : (c + 1) * ROWS, WIDTH : 2 * WIDTH] = rows_g
        for m in range(4):
            if c == 0 and m == 3:
                gat[0, rep, 48:64, :] = zmain[48:64, :]
                continue
            off = z_offset(c, m) if m < 3 else 8 + c
            send(
                zmain.at[c * ROWS + 16 * m : c * ROWS + 16 * m + 16, :],
                gat.at[c, rep, 16 * m : 16 * m + 16, :],
                zm_send, zm_recv.at[c], at_z(off),
            )

    def spread(part, to_blocks):
        r, t = iota((ROWS, 4 * ROWS), 0), iota((ROWS, 4 * ROWS), 1)
        place, block = (r & 15, r >> 4) if to_blocks else (r >> 2, r & 3)
        return (t == 16 * place + 4 * part + block).astype(F32).astype(BF16)

    def to_tiles(rows):
        tiles = None
        for part in range(4):
            one = dot(spread(part, False), rows[:, 128 * part : 128 * part + 128], (0, 0))
            tiles = one if part == 0 else tiles + one
        return tiles.astype(BF16)

    r = iota((ROWS, 1), 0)
    rows_h, rows_g = pick(code_of(r >> 2, 4), r & 3)
    zleft[...] = to_tiles(jnp.concatenate([rows_h, rows_g], axis=1))
    leftin[48:64, :] = zleft[48:64, :]

    def send_left(src, dst, ssem, rsem, sign):
        for c in range(4):
            for m in range(4):
                if c == 0 and m == 3:
                    continue
                off = z_offset(c, m) if m < 3 else 8 + c
                at = slice(16 * (4 * c + m), 16 * (4 * c + m) + 16)
                send(src.at[at, :], dst.at[at, :], ssem, rsem, at_z(off if sign > 0 else NZ - off))

    send_left(zleft, leftin, zl_send, zl_recv, 1)

    def gather(c):
        for ro in range(1, reps):
            send(gat.at[c, rep], gat.at[c, rep], c_send.at[c], c_recv.at[c], at_rep(ro))

    def arrive(c):
        here = 48 if isinstance(c, int) and c == 0 else ROWS
        wait(gat.at[c, rep, 0:here, :], zm_recv.at[c])
        gather(c)

    def arrive_left():
        wait(leftin.at[0:240], zl_recv)
        for part in range(4):
            gat[4, rep, :, 128 * part : 128 * part + 128] = dot(spread(part, False), leftin[...], (1, 0)).astype(BF16)
        gather(4)

    def compute(c):
        wait(gat.at[c, pl.ds(0, reps - 1)], c_recv.at[c])
        squares = None
        for s in range(reps):
            x = gat[c, s, :, 0:WIDTH].astype(F32)
            part = jnp.sum(x * x, axis=1, keepdims=True)
            squares = part if s == 0 else squares + part
        scale = 1.0 / jnp.sqrt(squares / features + EPSILON)
        hidden_grad = None
        for s in range(reps):
            cols = slice(WIDTH * s, WIDTH * s + WIDTH)
            x = gat[c, s, :, 0:WIDTH].astype(F32)
            nrm[c, :, cols] = (x * gain_ref[:, cols] * scale).astype(BF16)
            part = dot(gat[c, s, :, WIDTH : 2 * WIDTH], wd[:, cols], (1, 1))
            hidden_grad = part if s == 0 else hidden_grad + part
        gate_pre = dot(nrm[c], wg[...], (1, 1))
        up_pre = dot(nrm[c], wu[...], (1, 1))
        sig = jax.nn.sigmoid(gate_pre)
        activated = gate_pre * sig
        hidden = (activated * up_pre).astype(BF16)
        gate_grad = (hidden_grad * up_pre * sig * (1.0 + gate_pre * (1.0 - sig))).astype(BF16)
        up_grad = (hidden_grad * activated).astype(BF16)
        hid[c], ggr[c], ugr[c] = hidden, gate_grad, up_grad
        for s in range(reps):
            cols = slice(WIDTH * s, WIDTH * s + WIDTH)
            par[c, s, :, 0:WIDTH] = dot(hidden, wd[:, cols], (1, 0)).astype(BF16)
            par[c, s, :, WIDTH : 2 * WIDTH] = (
                dot(gate_grad, wg[:, cols], (1, 0)) + dot(up_grad, wu[:, cols], (1, 0))
            ).astype(BF16)
        for ro in range(1, reps):
            send(par.at[c, lax.rem(rep + ro, reps)], got.at[c, rep], e_send.at[c], e_recv.at[c], at_rep(ro))
        got[c, rep] = par[c, rep]

    def reduced(c):
        wait(got.at[c, pl.ds(0, reps - 1)], e_recv.at[c])
        total = got[c, 0].astype(F32)
        for s in range(1, reps):
            total = total + got[c, s].astype(F32)
        return total.astype(BF16)

    def back(c):
        start = pl.multiple_of(c * ROWS, ROWS)
        fmain[pl.ds(start, ROWS), :] = reduced(c)
        for m in range(4):
            at = pl.ds(pl.multiple_of(start + 16 * m, 16), 16)

            def far(at=at, m=m):
                off = z_offset(c, m) if m < 3 else 8 + c
                send(fmain.at[at, :], fmain_in.at[at, :], fm_send, fm_recv, at_z(NZ - off))

            if m < 3:
                far()
            else:
                pl.when(c > 0)(far)

    for copy in weights:
        copy.wait()
    arrive(0)
    arrive(1)

    def tick(t, carry):
        compute(t)

        @pl.when(t < 2)
        def _():
            arrive(t + 2)

        @pl.when(t == 2)
        def _():
            arrive_left()

        @pl.when(t > 0)
        def _():
            back(t - 1)

        return carry

    lax.fori_loop(0, CHUNKS, tick, 0)

    def turned(ref):
        return jnp.transpose(ref[...].reshape(CHUNKS * ROWS, ref.shape[2]).astype(F32)).astype(BF16)

    ht[...], ggt[...], ugt[...] = turned(hid), turned(ggr), turned(ugr)
    for s in range(reps):
        cols = slice(WIDTH * s, WIDTH * s + WIDTH)
        rows_n = nrm[:, :, cols].reshape(CHUNKS * ROWS, WIDTH)
        rows_g = gat[:, s, :, WIDTH : 2 * WIDTH].reshape(CHUNKS * ROWS, WIDTH)
        gu[:, cols] = dot(ggt[...], rows_n, (1, 0)).astype(BF16)
        uu[:, cols] = dot(ugt[...], rows_n, (1, 0)).astype(BF16)
        du[:, cols] = dot(ht[...], rows_g, (1, 0)).astype(BF16)
    updates = [
        pltpu.make_async_copy(gu, gu_hbm, o_sem.at[0]),
        pltpu.make_async_copy(uu, uu_hbm, o_sem.at[1]),
        pltpu.make_async_copy(du, du_hbm, o_sem.at[2]),
    ]
    for copy in updates:
        copy.start()

    fleft[...] = to_tiles(reduced(4))
    fleft_in[48:64, :] = fleft[48:64, :]
    send_left(fleft, fleft_in, fl_send, fl_recv, -1)

    fmain_in[48:64, :] = fmain[48:64, :]
    wait(fmain_in.at[0:240, :], fm_recv)
    r, t = iota((4 * ROWS, 4 * ROWS), 0), iota((4 * ROWS, 4 * ROWS), 1)
    regroup = (t == 16 * ((r >> 2) & 15) + 4 * (r >> 6) + (r & 3)).astype(F32).astype(BF16)
    main = dot(regroup, fmain_in[...], (1, 0)).astype(BF16)
    loc_in[0, 0:64, :] = main[0:64, :]
    for d in range(1, NJ):
        loc[d, 0:64, :] = main[64 * d : 64 * d + 64, :]
        send(loc.at[d, 0:64, :], loc_in.at[d, 0:64, :], l_send.at[0], l_recv.at[0, d], at_j_back(d))
    wait(fleft_in.at[0:240, :], fl_recv)
    for part in range(4):
        cols = slice(128 * part, 128 * part + 128)
        fifth = dot(spread(part, True), fleft_in[...], (1, 0)).astype(BF16)
        loc_in[0, 64:80, cols] = fifth[0:16, :]
        for d in range(1, NJ):
            loc[d, 64:80, cols] = fifth[16 * d : 16 * d + 16, :]
    for d in range(1, NJ):
        send(loc.at[d, 64:80, :], loc_in.at[d, 64:80, :], l_send.at[1], l_recv.at[1, d], at_j_back(d))

    r = iota((80, 1), 0)
    place = jnp.where(r < 64, r >> 2, r - 64)
    number = jnp.where(r < 64, r & 3, 4)
    plane = (z + offset_rows(place)) & (NZ - 1)
    for d in range(1, NJ):
        wait(loc_in.at[d, 0:64, :], l_recv.at[0, d])
        wait(loc_in.at[d, 64:80, :], l_recv.at[1, d])
    picked = [None, None]
    for d in range(NJ):
        code = ((plane * NJ + ((j + d) & (NJ - 1))) * 8 + number).astype(F32)
        for k in range(2):
            one = (code == meta[0, k : k + 1, :]).astype(F32).astype(BF16)
            part = dot(one, loc_in[d], (0, 0))
            picked[k] = part if d == 0 else picked[k] + part
    grad = g_ref[...].astype(F32)
    out_rows = [p[:, 0:WIDTH] for p in picked]
    share_out = (wcol_ref[:, 0:1] * out_rows[0] + wcol_ref[:, 1:2] * out_rows[1]).astype(BF16)
    share_in = (picked[0][:, WIDTH:] + picked[1][:, WIDTH:]).astype(BF16)
    dots = [jnp.sum(p * grad, axis=1, keepdims=True) for p in out_rows]
    high = [d.astype(BF16).astype(F32) for d in dots]
    lane = iota((128, WIDTH), 1)
    products = jnp.where(
        lane == 0, high[0],
        jnp.where(lane == 1, high[1], jnp.where(lane == 2, dots[0] - high[0], jnp.where(lane == 3, dots[1] - high[1], 0.0))),
    ).astype(BF16)
    for s in range(reps):
        rows = slice(share * s, share * s + share)
        fin[s, 0:share, :] = share_out[rows, :]
        fin[s, share : 2 * share, :] = share_in[rows, :]
        fin[s, 2 * share :, :] = products[rows, :]
    for ro in range(1, reps):
        send(fin.at[lax.rem(rep + ro, reps)], fin_in.at[rep], y_send, y_recv, at_rep(ro))
    fin_in[rep] = fin[rep]

    wait(hx.at[pl.ds(0, reps - 1)], hx_recv)
    squares = None
    for s in range(reps):
        x = hx[s].astype(F32)
        part = jnp.sum(x * x, axis=1, keepdims=True)
        squares = part if s == 0 else squares + part
    root = jnp.sqrt(squares / features + EPSILON)

    wait(fin_in.at[pl.ds(0, reps - 1)], y_recv)
    inner = route = None
    for s in range(reps):
        cols = slice(WIDTH * s, WIDTH * s + WIDTH)
        x = hx[s].astype(F32)
        lo_ref[:, cols] = (x + fin_in[s, 0:share, :].astype(F32)).astype(BF16)
        scaled = gain_ref[:, cols] * fin_in[s, share : 2 * share, :].astype(F32)
        part = jnp.sum(scaled * x, axis=1, keepdims=True)
        inner = part if s == 0 else inner + part
        part = fin_in[s, 2 * share :, 0:128].astype(F32)
        route = part if s == 0 else route + part
    coefficient = inner / (features * root * root * root)
    for s in range(reps):
        cols = slice(WIDTH * s, WIDTH * s + WIDTH)
        scaled = gain_ref[:, cols] * fin_in[s, share : 2 * share, :].astype(F32)
        ig_ref[:, cols] = (scaled / root - hx[s].astype(F32) * coefficient).astype(BF16)
    rg_ref[...] = route[:, 0:2] + route[:, 2:4]

    wait(meta.at[1:NJ], tok_send.at[0])
    wait(tokh.at[1:NJ], tok_send.at[1])
    wait(tokg.at[1:NJ], tok_send.at[2])
    wait(hx.at[pl.ds(0, reps - 1)], hx_send)
    wait(zmain.at[0:240, :], zm_send)
    wait(zleft.at[0:240, :], zl_send)
    for c in range(CHUNKS):
        wait(gat.at[c, pl.ds(0, reps - 1)], c_send.at[c])
        wait(got.at[c, pl.ds(0, reps - 1)], e_send.at[c])
    wait(fmain.at[0:240, :], fm_send)
    wait(fleft.at[0:240, :], fl_send)
    wait(loc.at[1:4, 0:64, :], l_send.at[0])
    wait(loc.at[1:4, 64:80, :], l_send.at[1])
    wait(fin.at[pl.ds(0, reps - 1)], y_send)
    for copy in updates:
        copy.wait()


def body(hidden_in, norm_gain, route_ids, route_weights, w_gate, w_up, w_down, out_grad):
    reps = lax.axis_size("rep")
    units, features = w_gate.shape[1:]
    tokens = hidden_in.shape[0]
    vmem = pl.BlockSpec(memory_space=pltpu.VMEM)
    hbm = pl.BlockSpec(memory_space=pl.ANY)
    matrix = pltpu.VMEM((units, features), BF16)
    dma = pltpu.SemaphoreType.DMA
    rows = CHUNKS * ROWS
    scratch = [matrix] * 6 + [
        pltpu.VMEM((NJ, tokens, WIDTH), BF16),
        pltpu.VMEM((NJ, tokens, WIDTH), BF16),
        pltpu.VMEM((NJ, 8, tokens), F32),
        pltpu.VMEM((reps, tokens // reps, WIDTH), BF16),
        pltpu.VMEM((4 * ROWS, 2 * WIDTH), BF16),
        pltpu.VMEM((4 * ROWS, 128), BF16),
        pltpu.VMEM((4 * ROWS, 128), BF16),
        pltpu.VMEM((CHUNKS, reps, ROWS, 2 * WIDTH), BF16),
        pltpu.VMEM((CHUNKS, ROWS, features), BF16),
        pltpu.VMEM((CHUNKS, reps, ROWS, 2 * WIDTH), BF16),
        pltpu.VMEM((CHUNKS, reps, ROWS, 2 * WIDTH), BF16),
        pltpu.VMEM((4 * ROWS, 2 * WIDTH), BF16),
        pltpu.VMEM((4 * ROWS, 128), BF16),
        pltpu.VMEM((4 * ROWS, 2 * WIDTH), BF16),
        pltpu.VMEM((4 * ROWS, 128), BF16),
        pltpu.VMEM((NJ, 80, 2 * WIDTH), BF16),
        pltpu.VMEM((NJ, 80, 2 * WIDTH), BF16),
        pltpu.VMEM((reps, 3 * (tokens // reps), WIDTH), BF16),
        pltpu.VMEM((reps, 3 * (tokens // reps), WIDTH), BF16),
    ]
    scratch += [pltpu.VMEM((CHUNKS, ROWS, units), BF16)] * 3
    scratch += [pltpu.VMEM((units, rows), BF16)] * 3
    scratch += [
        dma((3,)), dma((3,)),
        dma((3,)), dma((3, NJ)),
        dma, dma,
        dma, dma((4,)),
        dma, dma,
        dma((CHUNKS,)), dma((CHUNKS,)),
        dma((CHUNKS,)), dma((CHUNKS,)),
        dma, dma, dma, dma,
        dma((2,)), dma((2, NJ)),
        dma, dma,
    ]
    update = jax.ShapeDtypeStruct((units, features), BF16)
    outs = pl.pallas_call(
        kernel,
        out_shape=(
            jax.ShapeDtypeStruct((tokens // reps, features), BF16),
            jax.ShapeDtypeStruct((tokens // reps, features), BF16),
            jax.ShapeDtypeStruct((tokens // reps, 2), F32),
            update, update, update,
        ),
        in_specs=[vmem] * 6 + [hbm] * 3,
        out_specs=(vmem, vmem, vmem, hbm, hbm, hbm),
        scratch_shapes=scratch,
        compiler_params=pltpu.CompilerParams(
            collective_id=0, has_side_effects=True, vmem_limit_bytes=48 * 1024 * 1024
        ),
        name="expert_layer",
    )(
        hidden_in, out_grad, route_ids.T, route_weights.T, route_weights, norm_gain[None, :],
        w_gate[0], w_up[0], w_down[0],
    )
    layer_out, input_grad, route_grad, gate_update, up_update, down_update = outs
    return layer_out, input_grad, route_grad, gate_update[None], up_update[None], down_update[None]


def solution(mesh):
    placed = (
        P("exp", "rep"),
        P(),
        P("exp", None),
        P("exp", None),
        P("exp", "rep", None),
        P("exp", "rep", None),
        P("exp", "rep", None),
        P("exp", "rep"),
    )
    return jax.shard_map(
        body,
        mesh=mesh,
        in_specs=placed,
        out_specs=(
            P(("exp", "rep"), None),
            P(("exp", "rep"), None),
            P(("exp", "rep"), None),
            P("exp", "rep", None),
            P("exp", "rep", None),
            P("exp", "rep", None),
        ),
        check_vma=False,
    )
```

time: 610 us -> 123 us (0.20)
  waiting for transfers between devices: 405 us -> 0 us
  Pallas kernels: 0 us -> 110 us
  starting transfers between devices: 50.5 us -> 0 us
  blocking collectives: 48.3 us -> 0 us
  local copies, waits for them, and re-layouts: 49 us -> 9.62 us
  other arithmetic: 24.4 us -> 0 us
  matrix products: 13.7 us -> 0 us
  between operations: 14.1 us -> 0.71 us
    all_to_all x4 -> x0, waiting for transfers between devices: 332 us -> none  [the longest x1 92.8 us: body(): lax.all_to_all(send_grad, 'exp', split_axis=0, concat_axis=0, tiled=True)]
    pallas_call x0 -> x1, Pallas kernels: none -> 110 us  [body(): pl.pallas_call(kernel, out_shape=(jax.ShapeDtypeStruct((tokens // reps, f...]
    reduce_scatter x2 -> x0, waiting for transfers between devices: 72.3 us -> none  [the longest x1 45.8 us: body(): lax.psum_scatter(combined_out.astype(jnp.bfloat16), 'rep', scatter_dimens...]
    all_to_all x4 -> x0, starting transfers between devices: 50.2 us -> none  [the longest x1 25.8 us: body(): lax.all_to_all(send_normed, 'exp', split_axis=0, concat_axis=0, tiled=True)]
    all_gather x2 -> x0, blocking collectives: 48.3 us -> none  [the longest x1 24.9 us: body(): lax.all_gather(out_grad, 'rep', axis=1, tiled=True)]
    gather x12 -> x0, local copies, waits for them, and re-layouts: 20 us -> none  [the longest x2 5.41 us: fill_rows(): normed[token_safe]]
    all_to_all x6 -> x0, local copies, waits for them, and re-layouts: 18.2 us -> none  [the longest x2 5.97 us: body(): lax.all_to_all(input_part, 'exp', split_axis=0, concat_axis=0, tiled=True)]
    dot_general x9 -> x0, matrix products: 13.7 us -> none  [the longest x1 2.82 us: body(): lax.dot_general(rows_grad, down_matrix, contract_last, preferred_element_...]
  transfers between devices with their start and end apart: 7 -> 0, of which waited for: 6 -> 0; matrix products, arithmetic and copies ran while one was open for 7% -> 0% of each run, Pallas kernels for 0% -> 0%
where the time goes in v1:
time: 123 us; the launch traced here: 120 us
  Pallas kernels  110 us (89%)
  local copies, waits for them, and re-layouts  9.62 us (8%)
    pallas_call x1, Pallas kernels, body(): pl.pallas_call(kernel, out_shape=(jax.ShapeDtypeStruct((tokens // reps, f...  110 us
    unnamed x23, local copies, waits for them, and re-layouts  9.62 us

profile of v1, /device:TPU:1, one launch (start us, length us, event | category | flops | bytes accessed | tf_op | source)
XLA Modules:
  0.0 120.4 jit_solution(9460933376508113129)
XLA Ops:
  0.6 0.0 copy-start.3
  0.6 0.0 copy-start.5
  0.7 0.0 copy-start.6
  0.7 0.0 copy-start.7
  0.7 0.8 copy.14.wcol_ref
  1.5 0.0 copy-done.3
  1.5 0.0 copy-done.5
  1.5 0.0 copy-done.6
  1.5 0.0 copy-done.7
  1.5 0.0 copy-start
  1.6 1.1 copy-done
  2.7 0.0 copy-start.1
  2.7 1.1 copy-done.1
  3.8 0.0 copy-start.2
  3.8 1.1 copy-done.2
  5.0 0.0 copy-start.4
  5.0 0.8 copy-done.4
  5.8 110.1 %expert_layer.1 = (bf16[16,2048]{1,0:T(8,128)(2,1)S(1)}, bf16[16,2048]{1,0:T(8,128)(2,1)S(1)}, f32[16,2]{1,0:T(8,128)S(1)}, bf16[192,2048]{1,0:T(8,128)(2,1)S(1)...) custom-call(bf16[128,256]{1,0:T(8,128)(2,1)S(1)} %copy-done.3, bf16[128,256]{1,0:T(8,128)(2,1)S(1)} %copy-done.4, ...), custom_call_target="tpu_custom_call" | custom-call | tf_op jit(solution)/shard_map/expert_layer/pallas_call | solution.py:451
  115.9 0.6 copy.15
  116.5 0.6 copy.21
  117.2 0.6 copy.22
  117.8 0.9 copy.23
  118.7 0.9 copy.24
  119.5 0.9 copy.25
Async XLA Ops:
  0.6 0.9 copy-start.3
  0.6 0.9 copy-start.5
  0.7 0.9 copy-start.6
  0.7 0.9 copy-start.7
  1.5 1.1 copy-start
  2.7 1.1 copy-start.1
  3.8 1.1 copy-start.2
  5.0 0.8 copy-start.4

commit v2 on v1

v2 whole, which is shorter than its diff:
```python
import functools

import jax
import jax.numpy as jnp
from jax import lax
from jax.experimental import pallas as pl
from jax.experimental.pallas import tpu as pltpu
from jax.sharding import PartitionSpec as P

MESH = pl.DeviceIdType.MESH
EPSILON = 1e-06
NZ = 16
NJ = 4
WIDTH = 256
CHUNKS = 5
ROWS = 64
F32 = jnp.float32
BF16 = jnp.bfloat16


OFFSETS = (1, 15, 2, 0, 14, 3, 13, 4, 12, 5, 11, 8, 6, 10, 7, 9)
HOME = OFFSETS.index(0)


def choose(index, values):
    out = jnp.full_like(index, values[0])
    for i in range(1, len(values)):
        out = jnp.where(index == i, values[i], out)
    return out


def z_offset(c, m):
    if isinstance(c, int):
        return OFFSETS[4 * c + m]
    return choose(c, OFFSETS[m::4])


def iota(shape, dim):
    return lax.broadcasted_iota(jnp.int32, shape, dim)


def dot(a, b, dims):
    return lax.dot_general(a, b, ((dims[:1], dims[1:]), ((), ())), preferred_element_type=F32)


def kernel(
    h_hbm, g_hbm, ids_ref, wrow_ref, gain_ref, wg_hbm, wu_hbm, wd_hbm,
    lo_ref, ig_ref, rg_ref, gu_out, uu_out, du_out,
    wg, wu, wd, gu, uu, du,
    tok, meta, pickm, wpick, hx, zmain, zleft, leftin, gat, nrm, par, got, fmain, fleft,
    fmain_in, fleft_in, loc, loc_in, fin, fin_in, hid, ggr, ugr, ht, ggt, ugt,
    w_sem, o_sem, own_sem, meta_send, meta_recv, tok_send, tok_recv, hx_send, hx_recv,
    zm_send, zm_recv, zl_send, zl_recv, c_send, c_recv, e_send, e_recv,
    fm_send, fm_recv, fl_send, fl_recv, l_send, l_recv, y_send, y_recv,
):
    reps = lax.axis_size("rep")
    features = reps * WIDTH
    share = h_hbm.shape[0] // reps
    rep = lax.axis_index("rep")
    exp = lax.axis_index("exp")
    z, j = exp // NJ, exp % NJ
    columns = reps // 2
    x, y = rep // 2, rep % 2

    def at_z(off):
        return {"exp": lax.rem(z + off, NZ) * NJ + j}

    def in_plane(d):
        return lax.rem(j // 2 + d // 2, 2) * 2 + lax.rem(j % 2 + d % 2, 2)

    def at_j(d):
        return {"exp": z * NJ + in_plane(d)}

    def rid(dx, dy):
        return lax.rem(x + columns + dx, columns) * 2 + lax.rem(y + dy, 2)

    def at(dx, dy):
        return {"rep": rid(dx, dy)}

    def send(src, dst, ssem, rsem, device):
        pltpu.make_async_remote_copy(
            src_ref=src, dst_ref=dst, send_sem=ssem, recv_sem=rsem, device_id=device, device_id_type=MESH
        ).start()

    def wait(ref, sem):
        pltpu.make_async_copy(ref, ref, sem).wait()

    own = [
        pltpu.make_async_copy(h_hbm, tok.at[0, :, 0:WIDTH], own_sem.at[0]),
        pltpu.make_async_copy(g_hbm, tok.at[0, :, WIDTH : 2 * WIDTH], own_sem.at[1]),
    ]
    weights = [
        pltpu.make_async_copy(wg_hbm, wg, w_sem.at[0]),
        pltpu.make_async_copy(wu_hbm, wu, w_sem.at[1]),
        pltpu.make_async_copy(wd_hbm, wd, w_sem.at[2]),
    ]
    for copy in own + weights:
        copy.start()

    barrier = pltpu.get_barrier_semaphore()

    def greet(off, carry):
        pl.semaphore_signal(barrier, inc=1, device_id=at_z(off), device_id_type=MESH)
        return carry

    for d in range(1, NJ):
        pl.semaphore_signal(barrier, inc=1, device_id=at_j(d), device_id_type=MESH)
    lax.fori_loop(1, NZ, greet, 0)
    for ro in range(1, reps):
        pl.semaphore_signal(barrier, inc=1, device_id=at(ro // 2, ro % 2), device_id_type=MESH)

    ids = ids_ref[...]
    expert_rows = iota((NZ * NJ, 128), 0)
    hits = [(expert_rows == ids[k : k + 1, :]).astype(F32) for k in range(2)]
    before = (iota((128, 128), 0) < iota((128, 128), 1)).astype(F32).astype(BF16)
    earlier = dot((hits[0] + hits[1]).astype(BF16), before, (1, 0))
    for k in range(2):
        number = jnp.sum(hits[k] * earlier, axis=0, keepdims=True)
        meta[0, k : k + 1, :] = ids[k : k + 1, :].astype(F32) * 8.0 + number
    meta[0, 2:4, :] = wrow_ref[...]
    meta[0, 4:8, :] = jnp.zeros((4, 128), F32)

    for copy in own:
        copy.wait()
    pl.semaphore_wait(barrier, NZ - 1 + NJ - 1 + reps - 1)

    for d in (2, 3, 1):
        send(meta.at[0], meta.at[d], meta_send, meta_recv, at_j(d))
    for half in range(2):
        rows = slice(64 * half, 64 * half + 64)
        send(tok.at[0, rows, :], tok.at[2, rows, :], tok_send, tok_recv.at[half], at_j(2))
    send(tok.at[0], tok.at[1], tok_send, tok_recv.at[2], at_j(1))

    def code_of(place, number):
        plane = (z + choose(place, OFFSETS)) & (NZ - 1)
        return ((plane * NJ + j) * 8 + number).astype(F32)

    def pick(code, block, at_rows):
        weight = None
        for d in range(NJ):
            mine = jnp.where(block == d, code, -1.0)
            one = [mine == meta[d, k : k + 1, :] for k in range(2)]
            pickm[at_rows, 128 * d : 128 * d + 128] = (one[0] | one[1]).astype(F32).astype(BF16)
            w = jnp.sum(
                jnp.where(one[0], meta[d, 2:3, :], 0.0) + jnp.where(one[1], meta[d, 3:4, :], 0.0), axis=1, keepdims=True
            )
            weight = w if d == 0 else weight + w
        wpick[at_rows, :] = weight

    wait(meta.at[1:NJ], meta_recv)
    r = iota((ROWS, 1), 0)
    for c in range(4):
        pick(code_of(4 * c + (r >> 4), r & 3), (r >> 2) & 3, slice(c * ROWS, (c + 1) * ROWS))
    pick(code_of(r >> 2, 4), r & 3, slice(4 * ROWS, 5 * ROWS))

    for half in range(2):
        rows = slice(64 * half, 64 * half + 64)
        wait(tok.at[2, rows, :], tok_recv.at[half])
        send(tok.at[2, rows, :], tok.at[3, rows, :], tok_send, tok_recv.at[3 + half], at_j(1))
    wait(tok.at[1], tok_recv.at[2])
    for half in range(2):
        wait(tok.at[3, 64 * half : 64 * half + 64, :], tok_recv.at[3 + half])
    tokens = tok[...].reshape(NJ * tok.shape[1], 2 * WIDTH)

    def rows_of(at_rows):
        rows = dot(pickm[at_rows, :], tokens, (1, 0))
        return rows[:, 0:WIDTH].astype(BF16), (wpick[at_rows, :] * rows[:, WIDTH:]).astype(BF16)

    for c in range(4):
        rows_h, rows_g = rows_of(slice(c * ROWS, (c + 1) * ROWS))
        zmain[c * ROWS : (c + 1) * ROWS, 0:WIDTH] = rows_h
        zmain[c * ROWS : (c + 1) * ROWS, WIDTH : 2 * WIDTH] = rows_g
        for m in range(4):
            if 4 * c + m == HOME:
                gat[0, rep, 48:64, :] = zmain[48:64, :]
                continue
            send(
                zmain.at[c * ROWS + 16 * m : c * ROWS + 16 * m + 16, :],
                gat.at[c, rep, 16 * m : 16 * m + 16, :],
                zm_send, zm_recv.at[c], at_z(z_offset(c, m)),
            )

    def spread(part, to_blocks):
        r, t = iota((ROWS, 4 * ROWS), 0), iota((ROWS, 4 * ROWS), 1)
        place, block = (r & 15, r >> 4) if to_blocks else (r >> 2, r & 3)
        return (t == 16 * place + 4 * part + block).astype(F32).astype(BF16)

    def to_tiles(rows):
        tiles = None
        for part in range(4):
            one = dot(spread(part, False), rows[:, 128 * part : 128 * part + 128], (0, 0))
            tiles = one if part == 0 else tiles + one
        return tiles.astype(BF16)

    rows_h, rows_g = rows_of(slice(4 * ROWS, 5 * ROWS))
    zleft[...] = to_tiles(jnp.concatenate([rows_h, rows_g], axis=1))
    leftin[48:64, :] = zleft[48:64, :]

    def send_left(src, dst, ssem, rsem, sign):
        for place in range(16):
            if place == HOME:
                continue
            off = OFFSETS[place]
            rows = slice(16 * place, 16 * place + 16)
            send(src.at[rows, :], dst.at[rows, :], ssem, rsem, at_z(off if sign > 0 else NZ - off))

    send_left(zleft, leftin, zl_send, zl_recv, 1)

    for ro in range(1, reps):
        to = rid(ro // 2, ro % 2)
        rows = pl.ds(pl.multiple_of(to * share, 16), share)
        send(tok.at[0, rows, 0:WIDTH], hx.at[rep], hx_send, hx_recv, at(ro // 2, ro % 2))
    hx[rep] = tok[0, pl.ds(pl.multiple_of(rep * share, 16), share), 0:WIDTH]

    for copy in weights:
        copy.wait()

    low, high = slice(0, ROWS // 2), slice(ROWS // 2, ROWS)

    def gather(c):
        mine = gat.at[c, rep]
        send(mine, mine, c_send.at[c], c_recv.at[c, 0], at(0, 1))
        send(mine, mine, c_send.at[c], c_recv.at[c, 1], at(1, 0))
        send(mine, mine, c_send.at[c], c_recv.at[c, 2], at(-1, 0))

    def stage_0(c):
        @pl.when(c == 0)
        def _():
            wait(gat.at[c, rep, 0:48, :], zm_recv.at[0])
            gather(c)

        @pl.when((c > 0) & (c < 4))
        def _():
            wait(gat.at[c, rep], zm_recv.at[c])
            gather(c)

        @pl.when(c == 4)
        def _():
            wait(leftin.at[0:240, :], zl_recv)
            for part in range(4):
                cols = slice(128 * part, 128 * part + 128)
                gat[c, rep, :, cols] = dot(spread(part, False), leftin[...], (1, 0)).astype(BF16)
            gather(c)

    def stage_1(c):
        other, left, right = gat.at[c, rid(0, 1)], gat.at[c, rid(-1, 0)], gat.at[c, rid(1, 0)]
        wait(other, c_recv.at[c, 0])
        send(other, other, c_send.at[c], c_recv.at[c, 3], at(1, 0))
        send(other, other, c_send.at[c], c_recv.at[c, 4], at(-1, 0))
        wait(left, c_recv.at[c, 1])
        send(left.at[low, :], left.at[low, :], c_send.at[c], c_recv.at[c, 5], at(1, 0))
        wait(right, c_recv.at[c, 2])
        send(right.at[high, :], right.at[high, :], c_send.at[c], c_recv.at[c, 6], at(-1, 0))

    def stage_2(c):
        far = gat.at[c, rid(2, 0)]
        wait(far.at[low, :], c_recv.at[c, 5])
        wait(far.at[high, :], c_recv.at[c, 6])
        send(far, far, c_send.at[c], c_recv.at[c, 7], at(0, 1))

    def stage_3(c):
        wait(gat.at[c, rid(-1, 1)], c_recv.at[c, 3])
        wait(gat.at[c, rid(1, 1)], c_recv.at[c, 4])
        wait(gat.at[c, rid(2, 1)], c_recv.at[c, 7])
        squares = None
        for s in range(reps):
            v = gat[c, s, :, 0:WIDTH].astype(F32)
            part = jnp.sum(v * v, axis=1, keepdims=True)
            squares = part if s == 0 else squares + part
        scale = 1.0 / jnp.sqrt(squares / features + EPSILON)
        hidden_grad = None
        for s in range(reps):
            cols = slice(WIDTH * s, WIDTH * s + WIDTH)
            v = gat[c, s, :, 0:WIDTH].astype(F32)
            nrm[c, :, cols] = (v * gain_ref[:, cols] * scale).astype(BF16)
            part = dot(gat[c, s, :, WIDTH : 2 * WIDTH], wd[:, cols], (1, 1))
            hidden_grad = part if s == 0 else hidden_grad + part
        gate_pre = dot(nrm[c], wg[...], (1, 1))
        up_pre = dot(nrm[c], wu[...], (1, 1))
        sig = jax.nn.sigmoid(gate_pre)
        activated = gate_pre * sig
        hidden = (activated * up_pre).astype(BF16)
        gate_grad = (hidden_grad * up_pre * sig * (1.0 + gate_pre * (1.0 - sig))).astype(BF16)
        up_grad = (hidden_grad * activated).astype(BF16)
        hid[c], ggr[c], ugr[c] = hidden, gate_grad, up_grad
        for s in range(reps):
            cols = slice(WIDTH * s, WIDTH * s + WIDTH)
            par[c, s, :, 0:WIDTH] = dot(hidden, wd[:, cols], (1, 0)).astype(BF16)
            par[c, s, :, WIDTH : 2 * WIDTH] = (
                dot(gate_grad, wg[:, cols], (1, 0)) + dot(up_grad, wu[:, cols], (1, 0))
            ).astype(BF16)
        send(par.at[c, rid(2, 1)], got.at[c, 0], e_send.at[c], e_recv.at[c, 0], at(0, 1))
        send(par.at[c, rid(1, 1)], got.at[c, 1], e_send.at[c], e_recv.at[c, 1], at(1, 0))
        send(par.at[c, rid(-1, 1)], got.at[c, 2], e_send.at[c], e_recv.at[c, 2], at(-1, 0))

    def stage_4(c):
        far, other = rid(2, 0), rid(0, 1)
        wait(got.at[c, 0], e_recv.at[c, 0])
        par[c, far] = (par[c, far].astype(F32) + got[c, 0].astype(F32)).astype(BF16)
        send(par.at[c, far, low, :], got.at[c, 3, low, :], e_send.at[c], e_recv.at[c, 3], at(1, 0))
        send(par.at[c, far, high, :], got.at[c, 3, high, :], e_send.at[c], e_recv.at[c, 7], at(-1, 0))
        wait(got.at[c, 1], e_recv.at[c, 1])
        wait(got.at[c, 2], e_recv.at[c, 2])
        par[c, other] = (
            par[c, other].astype(F32) + got[c, 1].astype(F32) + got[c, 2].astype(F32)
        ).astype(BF16)
        send(par.at[c, other], got.at[c, 6], e_send.at[c], e_recv.at[c, 6], at(0, 1))

    def stage_5(c):
        right, left = rid(1, 0), rid(-1, 0)
        wait(got.at[c, 3, low, :], e_recv.at[c, 3])
        par[c, right, low, :] = (par[c, right, low, :].astype(F32) + got[c, 3, low, :].astype(F32)).astype(BF16)
        send(par.at[c, right], got.at[c, 4], e_send.at[c], e_recv.at[c, 4], at(1, 0))
        wait(got.at[c, 3, high, :], e_recv.at[c, 7])
        par[c, left, high, :] = (par[c, left, high, :].astype(F32) + got[c, 3, high, :].astype(F32)).astype(BF16)
        send(par.at[c, left], got.at[c, 5], e_send.at[c], e_recv.at[c, 5], at(-1, 0))

    def stage_6(c):
        total = par[c, rep].astype(F32)
        for k in (6, 4, 5):
            wait(got.at[c, k], e_recv.at[c, k])
            total = total + got[c, k].astype(F32)
        total = total.astype(BF16)

        @pl.when(c < 4)
        def _():
            start = pl.multiple_of(c * ROWS, ROWS)
            fmain[pl.ds(start, ROWS), :] = total
            for m in range(4):
                rows = pl.ds(pl.multiple_of(start + 16 * m, 16), 16)

                def far(rows=rows, m=m):
                    send(fmain.at[rows, :], fmain_in.at[rows, :], fm_send, fm_recv.at[c], at_z(NZ - z_offset(c, m)))

                if m == HOME:
                    pl.when(c > 0)(far)

                    @pl.when(c == 0)
                    def _():
                        fmain_in[48:64, :] = total[48:64, :]
                else:
                    far()

        @pl.when(c == 4)
        def _():
            tiles = to_tiles(total)
            fleft[...] = tiles
            fleft_in[48:64, :] = tiles[48:64, :]
            send_left(fleft, fleft_in, fl_send, fl_recv, -1)

    def to_blocks(c):
        rows = pl.ds(pl.multiple_of(16 * c, 16), 16)
        for d in range(1, NJ):
            send(loc.at[d, rows, :], loc_in.at[d, rows, :], l_send, l_recv, at_j(d))

    def stage_7(c):
        @pl.when(c < 4)
        def _():
            @pl.when(c == 0)
            def _():
                wait(fmain_in.at[0:48, :], fm_recv.at[0])

            @pl.when(c > 0)
            def _():
                wait(fmain_in.at[0:64, :], fm_recv.at[c])

            r, t = iota((ROWS, ROWS), 0), iota((ROWS, ROWS), 1)
            regroup = (t == 16 * ((r >> 2) & 3) + 4 * (r >> 4) + (r & 3)).astype(F32).astype(BF16)
            back = fmain_in[pl.ds(pl.multiple_of(c * ROWS, ROWS), ROWS), :]
            main = dot(regroup, back, (1, 0)).astype(BF16)
            rows = pl.ds(pl.multiple_of(16 * c, 16), 16)
            loc_in[0, rows, :] = main[0:16, :]
            for d in range(1, NJ):
                loc[d, rows, :] = main[16 * d : 16 * d + 16, :]
            to_blocks(c)

        @pl.when(c == 4)
        def _():
            wait(fleft_in.at[0:240, :], fl_recv)
            for part in range(4):
                cols = slice(128 * part, 128 * part + 128)
                fifth = dot(spread(part, True), fleft_in[...], (1, 0)).astype(BF16)
                loc_in[0, 64:80, cols] = fifth[0:16, :]
                for d in range(1, NJ):
                    loc[d, 64:80, cols] = fifth[16 * d : 16 * d + 16, :]
            to_blocks(c)

    def turned(ref):
        return jnp.transpose(ref[...].reshape(CHUNKS * ROWS, ref.shape[2]).astype(F32)).astype(BF16)

    def update(s):
        cols = pl.ds(pl.multiple_of(s * WIDTH, WIDTH), WIDTH)
        rows_n = nrm[:, :, cols].reshape(CHUNKS * ROWS, WIDTH)
        rows_g = gat[:, s, :, WIDTH : 2 * WIDTH].reshape(CHUNKS * ROWS, WIDTH)
        gu[:, cols] = dot(ggt[...], rows_n, (1, 0)).astype(BF16)
        uu[:, cols] = dot(ugt[...], rows_n, (1, 0)).astype(BF16)
        du[:, cols] = dot(ht[...], rows_g, (1, 0)).astype(BF16)

    stages = (
        (9, stage_7), (6, stage_6), (5, stage_5), (4, stage_4), (3, stage_3), (2, stage_2), (1, stage_1), (0, stage_0)
    )
    first_free = CHUNKS + 3
    ticks = CHUNKS + stages[0][0]
    per_tick = 2

    def tick(t, carry):
        for lag, stage in stages:
            pl.when((t >= lag) & (t - lag < CHUNKS))(functools.partial(stage, t - lag))

        @pl.when(t == first_free)
        def _():
            ht[...], ggt[...], ugt[...] = turned(hid), turned(ggr), turned(ugr)

        @pl.when((t >= first_free) & (t < first_free + reps // per_tick))
        def _():
            for s in range(per_tick):
                update((t - first_free) * per_tick + s)

        return carry

    lax.fori_loop(0, ticks, tick, 0)

    updates = [
        pltpu.make_async_copy(gu, gu_out, o_sem.at[0]),
        pltpu.make_async_copy(uu, uu_out, o_sem.at[1]),
        pltpu.make_async_copy(du, du_out, o_sem.at[2]),
    ]
    for copy in updates:
        copy.start()

    r = iota((80, 1), 0)
    place = jnp.where(r < 64, r >> 2, r - 64)
    number = jnp.where(r < 64, r & 3, 4)
    plane = (z + choose(place, OFFSETS)) & (NZ - 1)
    codes = [((plane * NJ + in_plane(d)) * 8 + number).astype(F32) for d in range(NJ)]
    ones = [
        jnp.concatenate([(code == meta[0, k : k + 1, :]).astype(F32).astype(BF16) for code in codes], axis=0)
        for k in range(2)
    ]
    grad = tok[0, :, WIDTH:].astype(F32)
    diagonal = iota((128, 128), 0) == iota((128, 128), 1)
    w = [jnp.sum(jnp.where(diagonal, meta[0, 2 + k : 3 + k, :], 0.0), axis=1, keepdims=True) for k in range(2)]
    wait(hx.at[pl.ds(0, reps - 1)], hx_recv)
    squares = None
    for s in range(reps):
        v = hx[s].astype(F32)
        part = jnp.sum(v * v, axis=1, keepdims=True)
        squares = part if s == 0 else squares + part
    root = jnp.sqrt(squares / features + EPSILON)

    wait(loc_in.at[1:NJ], l_recv)
    rows = loc_in[...].reshape(NJ * 80, 2 * WIDTH)
    picked = [dot(one, rows, (0, 0)) for one in ones]
    out_rows = [p[:, 0:WIDTH] for p in picked]
    share_out = (w[0] * out_rows[0] + w[1] * out_rows[1]).astype(BF16)
    share_in = (picked[0][:, WIDTH:] + picked[1][:, WIDTH:]).astype(BF16)
    dots = [jnp.sum(p * grad, axis=1, keepdims=True) for p in out_rows]
    heads = [d.astype(BF16).astype(F32) for d in dots]
    lane = iota((128, WIDTH), 1)
    products = jnp.where(
        lane == 0, heads[0],
        jnp.where(lane == 1, heads[1], jnp.where(lane == 2, dots[0] - heads[0], jnp.where(lane == 3, dots[1] - heads[1], 0.0))),
    ).astype(BF16)
    for s in range(reps):
        rows = slice(share * s, share * s + share)
        fin[s, 0:share, :] = share_out[rows, :]
        fin[s, share : 2 * share, :] = share_in[rows, :]
        fin[s, 2 * share :, :] = products[rows, :]
    for ro in range(1, reps):
        send(fin.at[rid(ro // 2, ro % 2)], fin_in.at[rep], y_send, y_recv, at(ro // 2, ro % 2))
    fin_in[rep] = fin[rep]

    wait(fin_in.at[pl.ds(0, reps - 1)], y_recv)
    inner = route = None
    for s in range(reps):
        cols = slice(WIDTH * s, WIDTH * s + WIDTH)
        v = hx[s].astype(F32)
        lo_ref[:, cols] = (v + fin_in[s, 0:share, :].astype(F32)).astype(BF16)
        scaled = gain_ref[:, cols] * fin_in[s, share : 2 * share, :].astype(F32)
        part = jnp.sum(scaled * v, axis=1, keepdims=True)
        inner = part if s == 0 else inner + part
        part = fin_in[s, 2 * share :, 0:128].astype(F32)
        route = part if s == 0 else route + part
    coefficient = inner / (features * root * root * root)
    for s in range(reps):
        cols = slice(WIDTH * s, WIDTH * s + WIDTH)
        scaled = gain_ref[:, cols] * fin_in[s, share : 2 * share, :].astype(F32)
        ig_ref[:, cols] = (scaled / root - hx[s].astype(F32) * coefficient).astype(BF16)
    diagonal = iota((share, share), 0) == iota((share, share), 1)
    for k in range(2):
        column = route[:, k : k + 1] + route[:, 2 + k : 3 + k]
        rg_ref[k : k + 1, :] = jnp.sum(jnp.where(diagonal, column, 0.0), axis=0, keepdims=True)

    wait(meta.at[1:NJ], meta_send)
    wait(tok.at[1:NJ], tok_send)
    wait(hx.at[pl.ds(0, reps - 1)], hx_send)
    wait(zmain.at[0:240, :], zm_send)
    wait(zleft.at[0:240, :], zl_send)
    for c in range(CHUNKS):
        wait(gat.at[c, pl.ds(0, 7)], c_send.at[c])
        wait(got.at[c], e_send.at[c])
    wait(fmain.at[0:240, :], fm_send)
    wait(fleft.at[0:240, :], fl_send)
    wait(loc.at[1:NJ], l_send)
    wait(fin.at[pl.ds(0, reps - 1)], y_send)
    for copy in updates:
        copy.wait()


def hand_out(*refs):
    n = len(refs) // 2
    copies = [pltpu.make_async_copy(refs[i], refs[n + i], refs[2 * n].at[i]) for i in range(n)]
    for copy in copies:
        copy.start()
    for copy in copies:
        copy.wait()


def body(hidden_in, norm_gain, route_ids, route_weights, w_gate, w_up, w_down, out_grad):
    reps = lax.axis_size("rep")
    units, features = w_gate.shape[1:]
    tokens = hidden_in.shape[0]
    share = tokens // reps
    vmem = pl.BlockSpec(memory_space=pltpu.VMEM)
    hbm = pl.BlockSpec(memory_space=pltpu.HBM)
    anywhere = pl.BlockSpec(memory_space=pl.ANY)
    matrix = pltpu.VMEM((units, features), BF16)
    dma = pltpu.SemaphoreType.DMA
    rows = CHUNKS * ROWS
    scratch = [matrix] * 6 + [
        pltpu.VMEM((NJ, tokens, 2 * WIDTH), BF16),
        pltpu.VMEM((NJ, 8, tokens), F32),
        pltpu.VMEM((rows, NJ * tokens), BF16),
        pltpu.VMEM((rows, 1), F32),
        pltpu.VMEM((reps, share, WIDTH), BF16),
        pltpu.VMEM((4 * ROWS, 2 * WIDTH), BF16),
        pltpu.VMEM((4 * ROWS, 128), BF16),
        pltpu.VMEM((4 * ROWS, 128), BF16),
        pltpu.VMEM((CHUNKS, reps, ROWS, 2 * WIDTH), BF16),
        pltpu.VMEM((CHUNKS, ROWS, features), BF16),
        pltpu.VMEM((CHUNKS, reps, ROWS, 2 * WIDTH), BF16),
        pltpu.VMEM((CHUNKS, 7, ROWS, 2 * WIDTH), BF16),
        pltpu.VMEM((4 * ROWS, 2 * WIDTH), BF16),
        pltpu.VMEM((4 * ROWS, 128), BF16),
        pltpu.VMEM((4 * ROWS, 2 * WIDTH), BF16),
        pltpu.VMEM((4 * ROWS, 128), BF16),
        pltpu.VMEM((NJ, 80, 2 * WIDTH), BF16),
        pltpu.VMEM((NJ, 80, 2 * WIDTH), BF16),
        pltpu.VMEM((reps, 3 * share, WIDTH), BF16),
        pltpu.VMEM((reps, 3 * share, WIDTH), BF16),
    ]
    scratch += [pltpu.VMEM((CHUNKS, ROWS, units), BF16)] * 3
    scratch += [pltpu.VMEM((units, rows), BF16)] * 3
    scratch += [
        dma((3,)), dma((3,)), dma((2,)),
        dma, dma, dma, dma((5,)),
        dma, dma,
        dma, dma((4,)),
        dma, dma,
        dma((CHUNKS,)), dma((CHUNKS, 8)),
        dma((CHUNKS,)), dma((CHUNKS, 8)),
        dma, dma((4,)), dma, dma,
        dma, dma,
        dma, dma,
    ]
    update = jax.ShapeDtypeStruct((units, features), BF16)
    kinds = (
        jax.ShapeDtypeStruct((share, features), BF16),
        jax.ShapeDtypeStruct((share, features), BF16),
        jax.ShapeDtypeStruct((2, share), F32),
        update, update, update,
    )
    outs = pl.pallas_call(
        kernel,
        out_shape=kinds,
        in_specs=[hbm] * 2 + [vmem] * 3 + [hbm] * 3,
        out_specs=(vmem, vmem, vmem, anywhere, anywhere, anywhere),
        scratch_shapes=scratch,
        compiler_params=pltpu.CompilerParams(
            collective_id=0, has_side_effects=True, vmem_limit_bytes=62 * 1024 * 1024
        ),
        name="expert_layer",
    )(
        hidden_in, out_grad, route_ids.T, route_weights.T, norm_gain[None, :], w_gate[0], w_up[0], w_down[0]
    )
    outs = pl.pallas_call(
        hand_out,
        out_shape=kinds,
        in_specs=[vmem] * 6,
        out_specs=(anywhere,) * 6,
        scratch_shapes=[dma((6,))],
        name="results",
    )(*outs)
    layer_out, input_grad, route_grad, gate_update, up_update, down_update = outs
    return layer_out, input_grad, route_grad.T, gate_update[None], up_update[None], down_update[None]


def solution(mesh):
    placed = (
        P("exp", "rep"),
        P(),
        P("exp", None),
        P("exp", None),
        P("exp", "rep", None),
        P("exp", "rep", None),
        P("exp", "rep", None),
        P("exp", "rep"),
    )
    return jax.shard_map(
        body,
        mesh=mesh,
        in_specs=placed,
        out_specs=(
            P(("exp", "rep"), None),
            P(("exp", "rep"), None),
            P(("exp", "rep"), None),
            P("exp", "rep", None),
            P("exp", "rep", None),
            P("exp", "rep", None),
        ),
        check_vma=False,
    )
```

time: 123 us -> 98.2 us (0.80); the launches traced: 120 us -> 98 us
  Pallas kernels: 110 us -> 97.3 us
  local copies, waits for them, and re-layouts: 9.62 us -> 0 us
    pallas_call x1 -> x2, Pallas kernels: 110 us -> 97.3 us  [the longest x1 94.1 us: body(): pl.pallas_call(kernel, out_shape=kinds, in_specs=[hbm] * 2 + [vmem] * 3 +...]
    unnamed x23 -> x0, local copies, waits for them, and re-layouts: 9.62 us -> none
where the time goes in v2:
time: 98.2 us; the launch traced here: 98 us
  Pallas kernels  97.3 us (99%)
    pallas_call x1, Pallas kernels, body(): pl.pallas_call(kernel, out_shape=kinds, in_specs=[hbm] * 2 + [vmem] * 3 +...  94.1 us
    pallas_call x1, Pallas kernels, body(): pl.pallas_call(hand_out, out_shape=kinds, in_specs=[vmem] * 6, out_specs=...  3.17 us

profile of v2, /device:TPU:1, one launch (start us, length us, event | category | flops | bytes accessed | tf_op | source)
XLA Modules:
  0.0 98.0 jit_solution(14088958853720283129)
XLA Ops:
  0.6 94.1 %expert_layer.1 = (bf16[16,2048]{1,0:T(8,128)(2,1)}, bf16[16,2048]{1,0:T(8,128)(2,1)}, f32[2,16]{1,0:T(2,128)}, bf16[192,2048]{1,0:T(8,128)(2,1)}, bf16[192,2048]{1,0:T(8,128)(2,1)}, /*index=5*/bf16[192,2048]{1,0:T(8,128)(2,1)}) custom-call(bf16[128,256]{1,0:T(8,128)(2,1)} %h_hbm.1, bf16[128,256]{1,0:T(8,128)(2,1)} %g_hbm.1, s32[2,128]{1,0:T(2,128)} %bitcast.14, ...), custom_call_target="tpu_custom_call" | custom-call | tf_op jit(solution)/shard_map/expert_layer/pallas_call | solution.py:573
  94.8 3.2 %results.1 = (bf16[16,2048]{1,0:T(8,128)(2,1)}, bf16[16,2048]{1,0:T(8,128)(2,1)}, f32[2,16]{1,0:T(2,128)}, bf16[192,2048]{1,0:T(8,128)(2,1)}, bf16[192,2048]{1,0:T(8,128)(2,1)}, /*index=5*/bf16[192,2048]{1,0:T(8,128)(2,1)}) custom-call(bf16[16,2048]{1,0:T(8,128)(2,1)} %get-tuple-element.18.refs_0_, bf16[16,2048]{1,0:T(8,128)(2,1)} %get-tuple-element.19.refs_1_, ...), custom_call_target="tpu_custom_call" | custom-call | tf_op jit(solution)/shard_map/results/pallas_call | solution.py:586

commit v3 on v2

--- a/solution.py
+++ b/solution.py
@@ -13,13 +13,16 @@
 NJ = 4
 WIDTH = 256
 CHUNKS = 5
+FIFTH = 3
 ROWS = 64
 F32 = jnp.float32
 BF16 = jnp.bfloat16
 
 
-OFFSETS = (1, 15, 2, 0, 14, 3, 13, 4, 12, 5, 11, 8, 6, 10, 7, 9)
-HOME = OFFSETS.index(0)
+OFFSETS = ((1, 15, 2, 0), (12, 5, 11, 8), (6, 10, 7, 9), None, (14, 3, 13, 4))
+MAIN = tuple(c for c in range(CHUNKS) if c != FIFTH)
+ALL = sum((OFFSETS[c] for c in MAIN), ())
+HOME = ALL.index(0)
 
 
 def choose(index, values):
@@ -31,8 +34,8 @@
 
 def z_offset(c, m):
     if isinstance(c, int):
-        return OFFSETS[4 * c + m]
-    return choose(c, OFFSETS[m::4])
+        return OFFSETS[c][m]
+    return choose(c, [OFFSETS[i][m] if i != FIFTH else 0 for i in range(CHUNKS)])
 
 
 def iota(shape, dim):
@@ -47,11 +50,10 @@
     h_hbm, g_hbm, ids_ref, wrow_ref, gain_ref, wg_hbm, wu_hbm, wd_hbm,
     lo_ref, ig_ref, rg_ref, gu_out, uu_out, du_out,
     wg, wu, wd, gu, uu, du,
-    tok, meta, pickm, wpick, hx, zmain, zleft, leftin, gat, nrm, par, got, fmain, fleft,
-    fmain_in, fleft_in, loc, loc_in, fin, fin_in, hid, ggr, ugr, ht, ggt, ugt,
+    tok, meta, hx, zout, zin, gat, nrm, par, got, fout, fback, loc, rows_in, fin, fin_in,
+    hid, ggr, ugr, ht, ggt, ugt,
     w_sem, o_sem, own_sem, meta_send, meta_recv, tok_send, tok_recv, hx_send, hx_recv,
-    zm_send, zm_recv, zl_send, zl_recv, c_send, c_recv, e_send, e_recv,
-    fm_send, fm_recv, fl_send, fl_recv, l_send, l_recv, y_send, y_recv,
+    z_send, z_recv, c_send, c_recv, e_send, e_recv, f_send, f_recv, l_send, l_recv, y_send, y_recv,
 ):
     reps = lax.axis_size("rep")
     features = reps * WIDTH
@@ -62,14 +64,11 @@
     columns = reps // 2
     x, y = rep // 2, rep % 2
 
-    def at_z(off):
-        return {"exp": lax.rem(z + off, NZ) * NJ + j}
-
     def in_plane(d):
         return lax.rem(j // 2 + d // 2, 2) * 2 + lax.rem(j % 2 + d % 2, 2)
 
-    def at_j(d):
-        return {"exp": z * NJ + in_plane(d)}
+    def at_place(off, d):
+        return {"exp": lax.rem(z + off, NZ) * NJ + in_plane(d)}
 
     def rid(dx, dy):
         return lax.rem(x + columns + dx, columns) * 2 + lax.rem(y + dy, 2)
@@ -100,12 +99,10 @@
     barrier = pltpu.get_barrier_semaphore()
 
     def greet(off, carry):
-        pl.semaphore_signal(barrier, inc=1, device_id=at_z(off), device_id_type=MESH)
+        pl.semaphore_signal(barrier, inc=1, device_id={"exp": lax.rem(exp + off, NZ * NJ)}, device_id_type=MESH)
         return carry
 
-    for d in range(1, NJ):
-        pl.semaphore_signal(barrier, inc=1, device_id=at_j(d), device_id_type=MESH)
-    lax.fori_loop(1, NZ, greet, 0)
+    lax.fori_loop(1, NZ * NJ, greet, 0)
     for ro in range(1, reps):
         pl.semaphore_signal(barrier, inc=1, device_id=at(ro // 2, ro % 2), device_id_type=MESH)
 
@@ -122,68 +119,75 @@
 
     for copy in own:
         copy.wait()
-    pl.semaphore_wait(barrier, NZ - 1 + NJ - 1 + reps - 1)
+
+    def code_of(off, place, number):
+        plane = (z + off) & (NZ - 1)
+        return ((plane * NJ + choose(place, [in_plane(d) for d in range(NJ)])) * 8 + number).astype(F32)
+
+    r = iota((4 * ROWS, 1), 0)
+    part_of = (r >> 2) & 3
+    blocks = jnp.concatenate([tok[0, :, 128 * f : 128 * f + 128] for f in range(4)], axis=0)
+
+    def pick(code, d):
+        one = [code == meta[d, k : k + 1, :] for k in range(2)]
+        w = jnp.where(one[0], meta[d, 2:3, :], 0.0) + jnp.where(one[1], meta[d, 3:4, :], 0.0)
+        return (one[0] | one[1]).astype(F32), jnp.sum(w, axis=1, keepdims=True)
+
+    def build(c):
+        hit, weight = pick(code_of(choose(r >> 6, OFFSETS[c]), (r >> 4) & 3, r & 3), 0)
+        masks = jnp.concatenate([jnp.where(part_of == f, hit, 0.0) for f in range(4)], axis=1).astype(BF16)
+        tiles = dot(masks, blocks, (1, 0))
+        zout[c] = jnp.where(part_of >= 2, weight * tiles, tiles).astype(BF16)
+
+    build(0)
+    pl.semaphore_wait(barrier, NZ * NJ - 1 + reps - 1)
+
+    def send_tiles(src, dst, ssem, rsem, c, sign):
+        for m in range(4):
+            off = z_offset(c, m)
+            off = off if sign > 0 else NZ - off
+            for d in range(NJ):
+                rows = slice(64 * m + 16 * d, 64 * m + 16 * d + 16)
+
+                def far(rows=rows, d=d, off=off):
+                    send(src.at[c, rows, :], dst.at[c, rows, :], ssem.at[c], rsem.at[c], at_place(off, d))
+
+                if m == HOME and d == 0:
+                    if not isinstance(c, int):
+                        pl.when(c > 0)(far)
+                    elif c > 0:
+                        far()
+                else:
+                    far()
+
+    def send_fifth(src, dst, ssem, rsem, sign):
+        for place, off in enumerate(ALL):
+            if place != HOME:
+                rows = slice(16 * place, 16 * place + 16)
+                to = at_place(off if sign > 0 else NZ - off, 0)
+                send(src.at[FIFTH, rows, :], dst.at[FIFTH, rows, :], ssem.at[FIFTH], rsem.at[FIFTH], to)
+
+    own_tile = slice(64 * HOME, 64 * HOME + 16)
+    own_fifth = slice(16 * HOME, 16 * HOME + 16)
+    send_tiles(zout, zin, z_send, z_recv, 0, 1)
+    zin[0, own_tile, :] = zout[0, own_tile, :]
 
     for d in (2, 3, 1):
-        send(meta.at[0], meta.at[d], meta_send, meta_recv, at_j(d))
-    for half in range(2):
-        rows = slice(64 * half, 64 * half + 64)
-        send(tok.at[0, rows, :], tok.at[2, rows, :], tok_send, tok_recv.at[half], at_j(2))
-    send(tok.at[0], tok.at[1], tok_send, tok_recv.at[2], at_j(1))
-
-    def code_of(place, number):
-        plane = (z + choose(place, OFFSETS)) & (NZ - 1)
-        return ((plane * NJ + j) * 8 + number).astype(F32)
-
-    def pick(code, block, at_rows):
-        weight = None
-        for d in range(NJ):
-            mine = jnp.where(block == d, code, -1.0)
-            one = [mine == meta[d, k : k + 1, :] for k in range(2)]
-            pickm[at_rows, 128 * d : 128 * d + 128] = (one[0] | one[1]).astype(F32).astype(BF16)
-            w = jnp.sum(
-                jnp.where(one[0], meta[d, 2:3, :], 0.0) + jnp.where(one[1], meta[d, 3:4, :], 0.0), axis=1, keepdims=True
-            )
-            weight = w if d == 0 else weight + w
-        wpick[at_rows, :] = weight
-
-    wait(meta.at[1:NJ], meta_recv)
-    r = iota((ROWS, 1), 0)
-    for c in range(4):
-        pick(code_of(4 * c + (r >> 4), r & 3), (r >> 2) & 3, slice(c * ROWS, (c + 1) * ROWS))
-    pick(code_of(r >> 2, 4), r & 3, slice(4 * ROWS, 5 * ROWS))
-
-    for half in range(2):
-        rows = slice(64 * half, 64 * half + 64)
-        wait(tok.at[2, rows, :], tok_recv.at[half])
-        send(tok.at[2, rows, :], tok.at[3, rows, :], tok_send, tok_recv.at[3 + half], at_j(1))
-    wait(tok.at[1], tok_recv.at[2])
-    for half in range(2):
-        wait(tok.at[3, 64 * half : 64 * half + 64, :], tok_recv.at[3 + half])
-    tokens = tok[...].reshape(NJ * tok.shape[1], 2 * WIDTH)
-
-    def rows_of(at_rows):
-        rows = dot(pickm[at_rows, :], tokens, (1, 0))
-        return rows[:, 0:WIDTH].astype(BF16), (wpick[at_rows, :] * rows[:, WIDTH:]).astype(BF16)
-
-    for c in range(4):
-        rows_h, rows_g = rows_of(slice(c * ROWS, (c + 1) * ROWS))
-        zmain[c * ROWS : (c + 1) * ROWS, 0:WIDTH] = rows_h
-        zmain[c * ROWS : (c + 1) * ROWS, WIDTH : 2 * WIDTH] = rows_g
-        for m in range(4):
-            if 4 * c + m == HOME:
-                gat[0, rep, 48:64, :] = zmain[48:64, :]
-                continue
-            send(
-                zmain.at[c * ROWS + 16 * m : c * ROWS + 16 * m + 16, :],
-                gat.at[c, rep, 16 * m : 16 * m + 16, :],
-                zm_send, zm_recv.at[c], at_z(z_offset(c, m)),
-            )
+        send(meta.at[0], meta.at[d], meta_send, meta_recv, at_place(0, d))
+    send(tok.at[0], tok.at[2], tok_send, tok_recv.at[1], at_place(0, 2))
+    send(tok.at[0], tok.at[1], tok_send, tok_recv.at[0], at_place(0, 1))
+    for c in MAIN[1:]:
+        build(c)
+        send_tiles(zout, zin, z_send, z_recv, c, 1)
+
+    def hand_on():
+        wait(tok.at[2], tok_recv.at[1])
+        send(tok.at[2], tok.at[3], tok_send, tok_recv.at[2], at_place(0, 1))
 
     def spread(part, to_blocks):
         r, t = iota((ROWS, 4 * ROWS), 0), iota((ROWS, 4 * ROWS), 1)
-        place, block = (r & 15, r >> 4) if to_blocks else (r >> 2, r & 3)
-        return (t == 16 * place + 4 * part + block).astype(F32).astype(BF16)
+        tile, d = (r & 15, r >> 4) if to_blocks else (r >> 2, r & 3)
+        return (t == 16 * tile + 4 * part + d).astype(F32).astype(BF16)
 
     def to_tiles(rows):
         tiles = None
@@ -192,19 +196,23 @@
             tiles = one if part == 0 else tiles + one
         return tiles.astype(BF16)
 
-    rows_h, rows_g = rows_of(slice(4 * ROWS, 5 * ROWS))
-    zleft[...] = to_tiles(jnp.concatenate([rows_h, rows_g], axis=1))
-    leftin[48:64, :] = zleft[48:64, :]
-
-    def send_left(src, dst, ssem, rsem, sign):
-        for place in range(16):
-            if place == HOME:
-                continue
-            off = OFFSETS[place]
-            rows = slice(16 * place, 16 * place + 16)
-            send(src.at[rows, :], dst.at[rows, :], ssem, rsem, at_z(off if sign > 0 else NZ - off))
-
-    send_left(zleft, leftin, zl_send, zl_recv, 1)
+    def send_fifth_rows():
+        wait(meta.at[1:NJ], meta_recv)
+        wait(tok.at[1], tok_recv.at[0])
+        wait(tok.at[3], tok_recv.at[2])
+        r = iota((ROWS, 1), 0)
+        code = code_of(choose(r >> 2, ALL), jnp.zeros_like(r), jnp.full_like(r, 4))
+        rows = weight = None
+        for d in range(NJ):
+            hit, w = pick(jnp.where((r & 3) == d, code, -1.0), d)
+            one = dot(hit.astype(BF16), tok[d], (1, 0))
+            rows = one if d == 0 else rows + one
+            weight = w if d == 0 else weight + w
+        lanes = iota((1, 2 * WIDTH), 1)
+        tiles = to_tiles(jnp.where(lanes < WIDTH, rows, weight * rows).astype(BF16))
+        zout[FIFTH] = tiles
+        zin[FIFTH, own_fifth, :] = tiles[own_fifth, :]
+        send_fifth(zout, zin, z_send, z_recv, 1)
 
     for ro in range(1, reps):
         to = rid(ro // 2, ro % 2)
@@ -223,24 +231,24 @@
         send(mine, mine, c_send.at[c], c_recv.at[c, 1], at(1, 0))
         send(mine, mine, c_send.at[c], c_recv.at[c, 2], at(-1, 0))
 
+    def wait_tiles(ref, sem, c):
+        fewer = (c == 0) | (c == FIFTH)
+
+        @pl.when(fewer)
+        def _():
+            wait(ref.at[c, 0:240, :], sem.at[c])
+
+        @pl.when(jnp.logical_not(fewer))
+        def _():
+            wait(ref.at[c], sem.at[c])
+
     def stage_0(c):
-        @pl.when(c == 0)
-        def _():
-            wait(gat.at[c, rep, 0:48, :], zm_recv.at[0])
-            gather(c)
-
-        @pl.when((c > 0) & (c < 4))
-        def _():
-            wait(gat.at[c, rep], zm_recv.at[c])
-            gather(c)
-
-        @pl.when(c == 4)
-        def _():
-            wait(leftin.at[0:240, :], zl_recv)
-            for part in range(4):
-                cols = slice(128 * part, 128 * part + 128)
-                gat[c, rep, :, cols] = dot(spread(part, False), leftin[...], (1, 0)).astype(BF16)
-            gather(c)
+        wait_tiles(zin, z_recv, c)
+        tiles = zin[c]
+        for part in range(4):
+            cols = slice(128 * part, 128 * part + 128)
+            gat[c, rep, :, cols] = dot(spread(part, False), tiles, (1, 0)).astype(BF16)
+        gather(c)
 
     def stage_1(c):
         other, left, right = gat.at[c, rid(0, 1)], gat.at[c, rid(-1, 0)], gat.at[c, rid(1, 0)]
@@ -320,70 +328,43 @@
         for k in (6, 4, 5):
             wait(got.at[c, k], e_recv.at[c, k])
             total = total + got[c, k].astype(F32)
-        total = total.astype(BF16)
-
-        @pl.when(c < 4)
-        def _():
-            start = pl.multiple_of(c * ROWS, ROWS)
-            fmain[pl.ds(start, ROWS), :] = total
-            for m in range(4):
-                rows = pl.ds(pl.multiple_of(start + 16 * m, 16), 16)
-
-                def far(rows=rows, m=m):
-                    send(fmain.at[rows, :], fmain_in.at[rows, :], fm_send, fm_recv.at[c], at_z(NZ - z_offset(c, m)))
-
-                if m == HOME:
-                    pl.when(c > 0)(far)
-
-                    @pl.when(c == 0)
-                    def _():
-                        fmain_in[48:64, :] = total[48:64, :]
-                else:
-                    far()
-
-        @pl.when(c == 4)
-        def _():
-            tiles = to_tiles(total)
-            fleft[...] = tiles
-            fleft_in[48:64, :] = tiles[48:64, :]
-            send_left(fleft, fleft_in, fl_send, fl_recv, -1)
-
-    def to_blocks(c):
-        rows = pl.ds(pl.multiple_of(16 * c, 16), 16)
-        for d in range(1, NJ):
-            send(loc.at[d, rows, :], loc_in.at[d, rows, :], l_send, l_recv, at_j(d))
+        tiles = to_tiles(total.astype(BF16))
+        fout[c] = tiles
+
+        @pl.when(c != FIFTH)
+        def _():
+            send_tiles(fout, fback, f_send, f_recv, c, -1)
+
+        @pl.when(c == 0)
+        def _():
+            fback[0, own_tile, :] = tiles[own_tile, :]
+
+        @pl.when(c == FIFTH)
+        def _():
+            fback[FIFTH, own_fifth, :] = tiles[own_fifth, :]
+            send_fifth(fout, fback, f_send, f_recv, -1)
 
     def stage_7(c):
-        @pl.when(c < 4)
-        def _():
-            @pl.when(c == 0)
-            def _():
-                wait(fmain_in.at[0:48, :], fm_recv.at[0])
-
-            @pl.when(c > 0)
-            def _():
-                wait(fmain_in.at[0:64, :], fm_recv.at[c])
-
-            r, t = iota((ROWS, ROWS), 0), iota((ROWS, ROWS), 1)
-            regroup = (t == 16 * ((r >> 2) & 3) + 4 * (r >> 4) + (r & 3)).astype(F32).astype(BF16)
-            back = fmain_in[pl.ds(pl.multiple_of(c * ROWS, ROWS), ROWS), :]
-            main = dot(regroup, back, (1, 0)).astype(BF16)
-            rows = pl.ds(pl.multiple_of(16 * c, 16), 16)
-            loc_in[0, rows, :] = main[0:16, :]
-            for d in range(1, NJ):
-                loc[d, rows, :] = main[16 * d : 16 * d + 16, :]
-            to_blocks(c)
-
-        @pl.when(c == 4)
-        def _():
-            wait(fleft_in.at[0:240, :], fl_recv)
+        wait_tiles(fback, f_recv, c)
+        tiles = fback[c]
+
+        @pl.when(c != FIFTH)
+        def _():
             for part in range(4):
                 cols = slice(128 * part, 128 * part + 128)
-                fifth = dot(spread(part, True), fleft_in[...], (1, 0)).astype(BF16)
-                loc_in[0, 64:80, cols] = fifth[0:16, :]
+                rows_in[c, :, cols] = dot(spread(part, False), tiles, (1, 0)).astype(BF16)
+
+        @pl.when(c == FIFTH)
+        def _():
+            for part in range(4):
+                cols = slice(128 * part, 128 * part + 128)
+                rows = dot(spread(part, True), tiles, (1, 0)).astype(BF16)
+                rows_in[FIFTH, 0:16, cols] = rows[0:16, :]
                 for d in range(1, NJ):
-                    loc[d, 64:80, cols] = fifth[16 * d : 16 * d + 16, :]
-            to_blocks(c)
+                    loc[d, :, cols] = rows[16 * d : 16 * d + 16, :]
+            for d in range(1, NJ):
+                rows = slice(16 * d, 16 * d + 16)
+                send(loc.at[d], rows_in.at[FIFTH, rows, :], l_send, l_recv, at_place(0, d))
 
     def turned(ref):
         return jnp.transpose(ref[...].reshape(CHUNKS * ROWS, ref.shape[2]).astype(F32)).astype(BF16)
@@ -404,8 +385,10 @@
     per_tick = 2
 
     def tick(t, carry):
-        for lag, stage in stages:
+        for lag, stage in reversed(stages):
             pl.when((t >= lag) & (t - lag < CHUNKS))(functools.partial(stage, t - lag))
+        pl.when(t == 0)(hand_on)
+        pl.when(t == 1)(send_fifth_rows)
 
         @pl.when(t == first_free)
         def _():
@@ -428,11 +411,12 @@
     for copy in updates:
         copy.start()
 
-    r = iota((80, 1), 0)
-    place = jnp.where(r < 64, r >> 2, r - 64)
-    number = jnp.where(r < 64, r & 3, 4)
-    plane = (z + choose(place, OFFSETS)) & (NZ - 1)
-    codes = [((plane * NJ + in_plane(d)) * 8 + number).astype(F32) for d in range(NJ)]
+    r = iota((ROWS, 1), 0)
+    codes = [
+        code_of(choose(r & 15, ALL), r >> 4, jnp.full_like(r, 4)) if c == FIFTH
+        else code_of(choose(r >> 4, OFFSETS[c]), (r >> 2) & 3, r & 3)
+        for c in range(CHUNKS)
+    ]
     ones = [
         jnp.concatenate([(code == meta[0, k : k + 1, :]).astype(F32).astype(BF16) for code in codes], axis=0)
         for k in range(2)
@@ -448,8 +432,8 @@
         squares = part if s == 0 else squares + part
     root = jnp.sqrt(squares / features + EPSILON)
 
-    wait(loc_in.at[1:NJ], l_recv)
-    rows = loc_in[...].reshape(NJ * 80, 2 * WIDTH)
+    wait(rows_in.at[FIFTH, 16:64, :], l_recv)
+    rows = rows_in[...].reshape(CHUNKS * ROWS, 2 * WIDTH)
     picked = [dot(one, rows, (0, 0)) for one in ones]
     out_rows = [p[:, 0:WIDTH] for p in picked]
     share_out = (w[0] * out_rows[0] + w[1] * out_rows[1]).astype(BF16)
@@ -494,13 +478,13 @@
     wait(meta.at[1:NJ], meta_send)
     wait(tok.at[1:NJ], tok_send)
     wait(hx.at[pl.ds(0, reps - 1)], hx_send)
-    wait(zmain.at[0:240, :], zm_send)
-    wait(zleft.at[0:240, :], zl_send)
+    for c in range(CHUNKS):
+        sent = slice(0, 240 if c in (0, FIFTH) else 256)
+        wait(zout.at[c, sent, :], z_send.at[c])
+        wait(fout.at[c, sent, :], f_send.at[c])
     for c in range(CHUNKS):
         wait(gat.at[c, pl.ds(0, 7)], c_send.at[c])
         wait(got.at[c], e_send.at[c])
-    wait(fmain.at[0:240, :], fm_send)
-    wait(fleft.at[0:240, :], fl_send)
     wait(loc.at[1:NJ], l_send)
     wait(fin.at[pl.ds(0, reps - 1)], y_send)
     for copy in updates:
@@ -508,11 +492,19 @@
 
 
 def hand_out(*refs):
-    n = len(refs) // 2
-    copies = [pltpu.make_async_copy(refs[i], refs[n + i], refs[2 * n].at[i]) for i in range(n)]
-    for copy in copies:
-        copy.start()
-    for copy in copies:
+    n = (len(refs) - 2) // 3
+    sources, results, held, in_sem, out_sem = refs[:n], refs[n : 2 * n], refs[2 * n : 3 * n], refs[-2], refs[-1]
+    pieces = [(i, slice(96 * k, 96 * k + 96)) for i in range(3, n) for k in range(2)]
+    pieces += [(i, slice(None)) for i in range(3)]
+    arriving, leaving = [], []
+    for k, (i, rows) in enumerate(pieces):
+        arriving.append(pltpu.make_async_copy(sources[i].at[rows, :], held[i].at[rows, :], in_sem.at[k]))
+        arriving[-1].start()
+    for k, (i, rows) in enumerate(pieces):
+        arriving[k].wait()
+        leaving.append(pltpu.make_async_copy(held[i].at[rows, :], results[i].at[rows, :], out_sem.at[k]))
+        leaving[-1].start()
+    for copy in leaving:
         copy.wait()
 
 
@@ -530,22 +522,17 @@
     scratch = [matrix] * 6 + [
         pltpu.VMEM((NJ, tokens, 2 * WIDTH), BF16),
         pltpu.VMEM((NJ, 8, tokens), F32),
-        pltpu.VMEM((rows, NJ * tokens), BF16),
-        pltpu.VMEM((rows, 1), F32),
         pltpu.VMEM((reps, share, WIDTH), BF16),
-        pltpu.VMEM((4 * ROWS, 2 * WIDTH), BF16),
-        pltpu.VMEM((4 * ROWS, 128), BF16),
-        pltpu.VMEM((4 * ROWS, 128), BF16),
+        pltpu.VMEM((CHUNKS, 4 * ROWS, 128), BF16),
+        pltpu.VMEM((CHUNKS, 4 * ROWS, 128), BF16),
         pltpu.VMEM((CHUNKS, reps, ROWS, 2 * WIDTH), BF16),
         pltpu.VMEM((CHUNKS, ROWS, features), BF16),
         pltpu.VMEM((CHUNKS, reps, ROWS, 2 * WIDTH), BF16),
         pltpu.VMEM((CHUNKS, 7, ROWS, 2 * WIDTH), BF16),
-        pltpu.VMEM((4 * ROWS, 2 * WIDTH), BF16),
-        pltpu.VMEM((4 * ROWS, 128), BF16),
-        pltpu.VMEM((4 * ROWS, 2 * WIDTH), BF16),
-        pltpu.VMEM((4 * ROWS, 128), BF16),
-        pltpu.VMEM((NJ, 80, 2 * WIDTH), BF16),
-        pltpu.VMEM((NJ, 80, 2 * WIDTH), BF16),
+        pltpu.VMEM((CHUNKS, 4 * ROWS, 128), BF16),
+        pltpu.VMEM((CHUNKS, 4 * ROWS, 128), BF16),
+        pltpu.VMEM((NJ, 16, 2 * WIDTH), BF16),
+        pltpu.VMEM((CHUNKS, ROWS, 2 * WIDTH), BF16),
         pltpu.VMEM((reps, 3 * share, WIDTH), BF16),
         pltpu.VMEM((reps, 3 * share, WIDTH), BF16),
     ]
@@ -553,13 +540,12 @@
     scratch += [pltpu.VMEM((units, rows), BF16)] * 3
     scratch += [
         dma((3,)), dma((3,)), dma((2,)),
-        dma, dma, dma, dma((5,)),
+        dma, dma, dma, dma((3,)),
         dma, dma,
-        dma, dma((4,)),
-        dma, dma,
+        dma((CHUNKS,)), dma((CHUNKS,)),
         dma((CHUNKS,)), dma((CHUNKS, 8)),
         dma((CHUNKS,)), dma((CHUNKS, 8)),
-        dma, dma((4,)), dma, dma,
+        dma((CHUNKS,)), dma((CHUNKS,)),
         dma, dma,
         dma, dma,
     ]
@@ -586,9 +572,9 @@
     outs = pl.pallas_call(
         hand_out,
         out_shape=kinds,
-        in_specs=[vmem] * 6,
+        in_specs=[anywhere] * 6,
         out_specs=(anywhere,) * 6,
-        scratch_shapes=[dma((6,))],
+        scratch_shapes=[pltpu.VMEM(kind.shape, kind.dtype) for kind in kinds] + [dma((9,)), dma((9,))],
         name="results",
     )(*outs)
     layer_out, input_grad, route_grad, gate_update, up_update, down_update = outs

time: 98.2 us -> 96.1 us (0.979)
  Pallas kernels: 97.3 us -> 95.3 us
    pallas_call x1, Pallas kernels: 94.1 us -> 92.7 us  [body(): pl.pallas_call(kernel, out_shape=kinds, in_specs=[hbm] * 2 + [vmem] * 3 +...]
where the time goes in v3:
time: 96.1 us; the launch traced here: 95.9 us
  Pallas kernels  95.3 us (99%)
    pallas_call x1, Pallas kernels, body(): pl.pallas_call(kernel, out_shape=kinds, in_specs=[hbm] * 2 + [vmem] * 3 +...  92.7 us
    pallas_call x1, Pallas kernels, body(): pl.pallas_call(hand_out, out_shape=kinds, in_specs=[anywhere] * 6, out_sp...  2.58 us

profile of v3, /device:TPU:1, one launch (start us, length us, event | category | flops | bytes accessed | tf_op | source)
XLA Modules:
  0.0 95.9 jit_solution(6420870848735129382)
XLA Ops:
  0.6 92.7 %expert_layer.1 = (bf16[16,2048]{1,0:T(8,128)(2,1)}, bf16[16,2048]{1,0:T(8,128)(2,1)}, f32[2,16]{1,0:T(2,128)}, bf16[192,2048]{1,0:T(8,128)(2,1)}, bf16[192,2048]{1,0:T(8,128)(2,1)}, /*index=5*/bf16[192,2048]{1,0:T(8,128)(2,1)}) custom-call(bf16[128,256]{1,0:T(8,128)(2,1)} %h_hbm.1, bf16[128,256]{1,0:T(8,128)(2,1)} %g_hbm.1, s32[2,128]{1,0:T(2,128)} %bitcast.14, ...), custom_call_target="tpu_custom_call" | custom-call | tf_op jit(solution)/shard_map/expert_layer/pallas_call | solution.py:559
  93.3 2.6 %results.1 = (bf16[16,2048]{1,0:T(8,128)(2,1)}, bf16[16,2048]{1,0:T(8,128)(2,1)}, f32[2,16]{1,0:T(2,128)}, bf16[192,2048]{1,0:T(8,128)(2,1)}, bf16[192,2048]{1,0:T(8,128)(2,1)}, /*index=5*/bf16[192,2048]{1,0:T(8,128)(2,1)}) custom-call(bf16[16,2048]{1,0:T(8,128)(2,1)} %get-tuple-element.18.refs_0_, bf16[16,2048]{1,0:T(8,128)(2,1)} %get-tuple-element.19.refs_1_, ...), custom_call_target="tpu_custom_call" | custom-call | tf_op jit(solution)/shard_map/results/pallas_call | solution.py:572

commit v4 on v3

--- a/solution.py
+++ b/solution.py
@@ -7,22 +7,24 @@
 from jax.experimental.pallas import tpu as pltpu
 from jax.sharding import PartitionSpec as P
 
-MESH = pl.DeviceIdType.MESH
+LOGICAL = pl.DeviceIdType.LOGICAL
 EPSILON = 1e-06
 NZ = 16
 NJ = 4
 WIDTH = 256
 CHUNKS = 5
-FIFTH = 3
 ROWS = 64
 F32 = jnp.float32
 BF16 = jnp.bfloat16
 
 
-OFFSETS = ((1, 15, 2, 0), (12, 5, 11, 8), (6, 10, 7, 9), None, (14, 3, 13, 4))
+OFFSETS = ((0, 3, 13, 4), (7, 9, 8, 10), None, (5, 11, 6, 12), (1, 2, 14, 15))
+FIFTH = OFFSETS.index(None)
 MAIN = tuple(c for c in range(CHUNKS) if c != FIFTH)
 ALL = sum((OFFSETS[c] for c in MAIN), ())
-HOME = ALL.index(0)
+HOME = next(c for c in MAIN if 0 in OFFSETS[c])
+OWN_TILE = slice(64 * OFFSETS[HOME].index(0), 64 * OFFSETS[HOME].index(0) + 16)
+OWN_FIFTH = slice(16 * ALL.index(0), 16 * ALL.index(0) + 16)
 
 
 def choose(index, values):
@@ -50,7 +52,7 @@
     h_hbm, g_hbm, ids_ref, wrow_ref, gain_ref, wg_hbm, wu_hbm, wd_hbm,
     lo_ref, ig_ref, rg_ref, gu_out, uu_out, du_out,
     wg, wu, wd, gu, uu, du,
-    tok, meta, hx, zout, zin, gat, nrm, par, got, fout, fback, loc, rows_in, fin, fin_in,
+    tok, meta, hx, zout, zin, gat, nrm, par, got, fout, fback, loc, fifth_in, picked, fin, fin_in,
     hid, ggr, ugr, ht, ggt, ugt,
     w_sem, o_sem, own_sem, meta_send, meta_recv, tok_send, tok_recv, hx_send, hx_recv,
     z_send, z_recv, c_send, c_recv, e_send, e_recv, f_send, f_recv, l_send, l_recv, y_send, y_recv,
@@ -64,21 +66,30 @@
     columns = reps // 2
     x, y = rep // 2, rep % 2
 
+    here = rep * (NZ * NJ)
+    planes = [lax.rem(j // 2 + d // 2, 2) * 2 + lax.rem(j % 2 + d % 2, 2) for d in range(NJ)]
+    ids_z = [here + lax.rem(z + off, NZ) * NJ for off in range(NZ)]
+    slots = {
+        (dx, dy): lax.rem(x + columns + dx, columns) * 2 + lax.rem(y + dy, 2) for dx in (-1, 0, 1, 2) for dy in (0, 1)
+    }
+
     def in_plane(d):
-        return lax.rem(j // 2 + d // 2, 2) * 2 + lax.rem(j % 2 + d % 2, 2)
+        return planes[d]
 
     def at_place(off, d):
-        return {"exp": lax.rem(z + off, NZ) * NJ + in_plane(d)}
+        if isinstance(off, int):
+            return ids_z[off % NZ] + planes[d]
+        return here + lax.rem(z + off, NZ) * NJ + planes[d]
 
     def rid(dx, dy):
-        return lax.rem(x + columns + dx, columns) * 2 + lax.rem(y + dy, 2)
+        return slots[(dx + 1) % columns - 1, dy]
 
     def at(dx, dy):
-        return {"rep": rid(dx, dy)}
+        return rid(dx, dy) * (NZ * NJ) + exp
 
     def send(src, dst, ssem, rsem, device):
         pltpu.make_async_remote_copy(
-            src_ref=src, dst_ref=dst, send_sem=ssem, recv_sem=rsem, device_id=device, device_id_type=MESH
+            src_ref=src, dst_ref=dst, send_sem=ssem, recv_sem=rsem, device_id=device, device_id_type=LOGICAL
         ).start()
 
     def wait(ref, sem):
@@ -98,13 +109,14 @@
 
     barrier = pltpu.get_barrier_semaphore()
 
-    def greet(off, carry):
-        pl.semaphore_signal(barrier, inc=1, device_id={"exp": lax.rem(exp + off, NZ * NJ)}, device_id_type=MESH)
+    def greet(i, carry):
+        off = 1 + lax.rem(i + 20, NZ * NJ - 1)
+        pl.semaphore_signal(barrier, inc=1, device_id=here + lax.rem(exp + off, NZ * NJ), device_id_type=LOGICAL)
         return carry
 
-    lax.fori_loop(1, NZ * NJ, greet, 0)
+    lax.fori_loop(0, NZ * NJ - 1, greet, 0)
     for ro in range(1, reps):
-        pl.semaphore_signal(barrier, inc=1, device_id=at(ro // 2, ro % 2), device_id_type=MESH)
+        pl.semaphore_signal(barrier, inc=1, device_id=at(ro // 2, ro % 2), device_id_type=LOGICAL)
 
     ids = ids_ref[...]
     expert_rows = iota((NZ * NJ, 128), 0)
@@ -139,7 +151,7 @@
         tiles = dot(masks, blocks, (1, 0))
         zout[c] = jnp.where(part_of >= 2, weight * tiles, tiles).astype(BF16)
 
-    build(0)
+    build(MAIN[0])
     pl.semaphore_wait(barrier, NZ * NJ - 1 + reps - 1)
 
     def send_tiles(src, dst, ssem, rsem, c, sign):
@@ -152,25 +164,22 @@
                 def far(rows=rows, d=d, off=off):
                     send(src.at[c, rows, :], dst.at[c, rows, :], ssem.at[c], rsem.at[c], at_place(off, d))
 
-                if m == HOME and d == 0:
+                if OFFSETS[HOME][m] == 0 and d == 0:
                     if not isinstance(c, int):
-                        pl.when(c > 0)(far)
-                    elif c > 0:
+                        pl.when(c != HOME)(far)
+                    elif c != HOME:
                         far()
                 else:
                     far()
 
     def send_fifth(src, dst, ssem, rsem, sign):
         for place, off in enumerate(ALL):
-            if place != HOME:
+            if off != 0:
                 rows = slice(16 * place, 16 * place + 16)
                 to = at_place(off if sign > 0 else NZ - off, 0)
                 send(src.at[FIFTH, rows, :], dst.at[FIFTH, rows, :], ssem.at[FIFTH], rsem.at[FIFTH], to)
 
-    own_tile = slice(64 * HOME, 64 * HOME + 16)
-    own_fifth = slice(16 * HOME, 16 * HOME + 16)
-    send_tiles(zout, zin, z_send, z_recv, 0, 1)
-    zin[0, own_tile, :] = zout[0, own_tile, :]
+    send_tiles(zout, zin, z_send, z_recv, MAIN[0], 1)
 
     for d in (2, 3, 1):
         send(meta.at[0], meta.at[d], meta_send, meta_recv, at_place(0, d))
@@ -179,6 +188,7 @@
     for c in MAIN[1:]:
         build(c)
         send_tiles(zout, zin, z_send, z_recv, c, 1)
+    zin[HOME, OWN_TILE, :] = zout[HOME, OWN_TILE, :]
 
     def hand_on():
         wait(tok.at[2], tok_recv.at[1])
@@ -211,7 +221,7 @@
         lanes = iota((1, 2 * WIDTH), 1)
         tiles = to_tiles(jnp.where(lanes < WIDTH, rows, weight * rows).astype(BF16))
         zout[FIFTH] = tiles
-        zin[FIFTH, own_fifth, :] = tiles[own_fifth, :]
+        zin[FIFTH, OWN_FIFTH, :] = tiles[OWN_FIFTH, :]
         send_fifth(zout, zin, z_send, z_recv, 1)
 
     for ro in range(1, reps):
@@ -232,7 +242,7 @@
         send(mine, mine, c_send.at[c], c_recv.at[c, 2], at(-1, 0))
 
     def wait_tiles(ref, sem, c):
-        fewer = (c == 0) | (c == FIFTH)
+        fewer = (c == HOME) | (c == FIFTH)
 
         @pl.when(fewer)
         def _():
@@ -335,14 +345,19 @@
         def _():
             send_tiles(fout, fback, f_send, f_recv, c, -1)
 
-        @pl.when(c == 0)
-        def _():
-            fback[0, own_tile, :] = tiles[own_tile, :]
+        @pl.when(c == HOME)
+        def _():
+            fback[HOME, OWN_TILE, :] = tiles[OWN_TILE, :]
 
         @pl.when(c == FIFTH)
         def _():
-            fback[FIFTH, own_fifth, :] = tiles[own_fifth, :]
+            fback[FIFTH, OWN_FIFTH, :] = tiles[OWN_FIFTH, :]
             send_fifth(fout, fback, f_send, f_recv, -1)
+
+    def add_rows(code, rows):
+        for k in range(2):
+            one = (code == meta[0, k : k + 1, :]).astype(F32).astype(BF16)
+            picked[k] = picked[k] + dot(one, rows, (0, 0))
 
     def stage_7(c):
         wait_tiles(fback, f_recv, c)
@@ -350,21 +365,22 @@
 
         @pl.when(c != FIFTH)
         def _():
-            for part in range(4):
-                cols = slice(128 * part, 128 * part + 128)
-                rows_in[c, :, cols] = dot(spread(part, False), tiles, (1, 0)).astype(BF16)
+            rows = [dot(spread(part, False), tiles, (1, 0)).astype(BF16) for part in range(4)]
+            r = iota((ROWS, 1), 0)
+            code = code_of(choose(r >> 4, [z_offset(c, m) for m in range(4)]), (r >> 2) & 3, r & 3)
+            add_rows(code, jnp.concatenate(rows, axis=1))
 
         @pl.when(c == FIFTH)
         def _():
             for part in range(4):
                 cols = slice(128 * part, 128 * part + 128)
                 rows = dot(spread(part, True), tiles, (1, 0)).astype(BF16)
-                rows_in[FIFTH, 0:16, cols] = rows[0:16, :]
+                fifth_in[0:16, cols] = rows[0:16, :]
                 for d in range(1, NJ):
                     loc[d, :, cols] = rows[16 * d : 16 * d + 16, :]
             for d in range(1, NJ):
                 rows = slice(16 * d, 16 * d + 16)
-                send(loc.at[d], rows_in.at[FIFTH, rows, :], l_send, l_recv, at_place(0, d))
+                send(loc.at[d], fifth_in.at[rows, :], l_send, l_recv, at_place(0, d))
 
     def turned(ref):
         return jnp.transpose(ref[...].reshape(CHUNKS * ROWS, ref.shape[2]).astype(F32)).astype(BF16)
@@ -387,8 +403,6 @@
     def tick(t, carry):
         for lag, stage in reversed(stages):
             pl.when((t >= lag) & (t - lag < CHUNKS))(functools.partial(stage, t - lag))
-        pl.when(t == 0)(hand_on)
-        pl.when(t == 1)(send_fifth_rows)
 
         @pl.when(t == first_free)
         def _():
@@ -401,6 +415,9 @@
 
         return carry
 
+    picked[...] = jnp.zeros_like(picked)
+    hand_on()
+    send_fifth_rows()
     lax.fori_loop(0, ticks, tick, 0)
 
     updates = [
@@ -411,16 +428,6 @@
     for copy in updates:
         copy.start()
 
-    r = iota((ROWS, 1), 0)
-    codes = [
-        code_of(choose(r & 15, ALL), r >> 4, jnp.full_like(r, 4)) if c == FIFTH
-        else code_of(choose(r >> 4, OFFSETS[c]), (r >> 2) & 3, r & 3)
-        for c in range(CHUNKS)
-    ]
-    ones = [
-        jnp.concatenate([(code == meta[0, k : k + 1, :]).astype(F32).astype(BF16) for code in codes], axis=0)
-        for k in range(2)
-    ]
     grad = tok[0, :, WIDTH:].astype(F32)
     diagonal = iota((128, 128), 0) == iota((128, 128), 1)
     w = [jnp.sum(jnp.where(diagonal, meta[0, 2 + k : 3 + k, :], 0.0), axis=1, keepdims=True) for k in range(2)]
@@ -432,44 +439,48 @@
         squares = part if s == 0 else squares + part
     root = jnp.sqrt(squares / features + EPSILON)
 
-    wait(rows_in.at[FIFTH, 16:64, :], l_recv)
-    rows = rows_in[...].reshape(CHUNKS * ROWS, 2 * WIDTH)
-    picked = [dot(one, rows, (0, 0)) for one in ones]
-    out_rows = [p[:, 0:WIDTH] for p in picked]
+    r = iota((ROWS, 1), 0)
+    code = code_of(choose(r & 15, ALL), r >> 4, jnp.full_like(r, 4))
+    wait(fifth_in.at[16:64, :], l_recv)
+    add_rows(code, fifth_in[...])
+    out_rows = [picked[k, :, 0:WIDTH] for k in range(2)]
     share_out = (w[0] * out_rows[0] + w[1] * out_rows[1]).astype(BF16)
-    share_in = (picked[0][:, WIDTH:] + picked[1][:, WIDTH:]).astype(BF16)
+    share_in = (picked[0, :, WIDTH:] + picked[1, :, WIDTH:]).astype(BF16)
     dots = [jnp.sum(p * grad, axis=1, keepdims=True) for p in out_rows]
     heads = [d.astype(BF16).astype(F32) for d in dots]
-    lane = iota((128, WIDTH), 1)
+    lane = iota((128, 128), 1)
     products = jnp.where(
         lane == 0, heads[0],
         jnp.where(lane == 1, heads[1], jnp.where(lane == 2, dots[0] - heads[0], jnp.where(lane == 3, dots[1] - heads[1], 0.0))),
     ).astype(BF16)
+    halves = [share_out[:, 0:128], share_out[:, 128:], share_in[:, 0:128], share_in[:, 128:], products]
     for s in range(reps):
-        rows = slice(share * s, share * s + share)
-        fin[s, 0:share, :] = share_out[rows, :]
-        fin[s, share : 2 * share, :] = share_in[rows, :]
-        fin[s, 2 * share :, :] = products[rows, :]
+        for i, half in enumerate(halves):
+            fin[s, share * i : share * i + share, :] = half[share * s : share * s + share, :]
     for ro in range(1, reps):
         send(fin.at[rid(ro // 2, ro % 2)], fin_in.at[rep], y_send, y_recv, at(ro // 2, ro % 2))
     fin_in[rep] = fin[rep]
 
     wait(fin_in.at[pl.ds(0, reps - 1)], y_recv)
     inner = route = None
-    for s in range(reps):
-        cols = slice(WIDTH * s, WIDTH * s + WIDTH)
-        v = hx[s].astype(F32)
-        lo_ref[:, cols] = (v + fin_in[s, 0:share, :].astype(F32)).astype(BF16)
-        scaled = gain_ref[:, cols] * fin_in[s, share : 2 * share, :].astype(F32)
+    for s in range(2 * reps):
+        cols = slice(128 * s, 128 * s + 128)
+        v = hx[s // 2, :, 128 * (s % 2) : 128 * (s % 2) + 128].astype(F32)
+        at_out, at_in = share * (s % 2), share * (2 + s % 2)
+        lo_ref[:, cols] = (v + fin_in[s // 2, at_out : at_out + share, :].astype(F32)).astype(BF16)
+        scaled = gain_ref[:, cols] * fin_in[s // 2, at_in : at_in + share, :].astype(F32)
         part = jnp.sum(scaled * v, axis=1, keepdims=True)
         inner = part if s == 0 else inner + part
-        part = fin_in[s, 2 * share :, 0:128].astype(F32)
+    for s in range(reps):
+        part = fin_in[s, 4 * share :, :].astype(F32)
         route = part if s == 0 else route + part
     coefficient = inner / (features * root * root * root)
-    for s in range(reps):
-        cols = slice(WIDTH * s, WIDTH * s + WIDTH)
-        scaled = gain_ref[:, cols] * fin_in[s, share : 2 * share, :].astype(F32)
-        ig_ref[:, cols] = (scaled / root - hx[s].astype(F32) * coefficient).astype(BF16)
+    for s in range(2 * reps):
+        cols = slice(128 * s, 128 * s + 128)
+        v = hx[s // 2, :, 128 * (s % 2) : 128 * (s % 2) + 128].astype(F32)
+        at_in = share * (2 + s % 2)
+        scaled = gain_ref[:, cols] * fin_in[s // 2, at_in : at_in + share, :].astype(F32)
+        ig_ref[:, cols] = (scaled / root - v * coefficient).astype(BF16)
     diagonal = iota((share, share), 0) == iota((share, share), 1)
     for k in range(2):
         column = route[:, k : k + 1] + route[:, 2 + k : 3 + k]
@@ -479,7 +490,7 @@
     wait(tok.at[1:NJ], tok_send)
     wait(hx.at[pl.ds(0, reps - 1)], hx_send)
     for c in range(CHUNKS):
-        sent = slice(0, 240 if c in (0, FIFTH) else 256)
+        sent = slice(0, 240 if c in (HOME, FIFTH) else 256)
         wait(zout.at[c, sent, :], z_send.at[c])
         wait(fout.at[c, sent, :], f_send.at[c])
     for c in range(CHUNKS):
@@ -532,9 +543,10 @@
         pltpu.VMEM((CHUNKS, 4 * ROWS, 128), BF16),
         pltpu.VMEM((CHUNKS, 4 * ROWS, 128), BF16),
         pltpu.VMEM((NJ, 16, 2 * WIDTH), BF16),
-        pltpu.VMEM((CHUNKS, ROWS, 2 * WIDTH), BF16),
-        pltpu.VMEM((reps, 3 * share, WIDTH), BF16),
-        pltpu.VMEM((reps, 3 * share, WIDTH), BF16),
+        pltpu.VMEM((ROWS, 2 * WIDTH), BF16),
+        pltpu.VMEM((2, tokens, 2 * WIDTH), F32),
+        pltpu.VMEM((reps, 5 * share, 128), BF16),
+        pltpu.VMEM((reps, 5 * share, 128), BF16),
     ]
     scratch += [pltpu.VMEM((CHUNKS, ROWS, units), BF16)] * 3
     scratch += [pltpu.VMEM((units, rows), BF16)] * 3

time: 96.1 us -> 94.2 us (0.980)
  Pallas kernels: 95.3 us -> 93.4 us
    pallas_call x1, Pallas kernels: 92.7 us -> 90.8 us  [body(): pl.pallas_call(kernel, out_shape=kinds, in_specs=[hbm] * 2 + [vmem] * 3 +...]
where the time goes in v4:
time: 94.2 us; the launch traced here: 94 us
  Pallas kernels  93.4 us (99%)
    pallas_call x1, Pallas kernels, body(): pl.pallas_call(kernel, out_shape=kinds, in_specs=[hbm] * 2 + [vmem] * 3 +...  90.8 us
    pallas_call x1, Pallas kernels, body(): pl.pallas_call(hand_out, out_shape=kinds, in_specs=[anywhere] * 6, out_sp...  2.58 us

profile of v4, /device:TPU:1, one launch (start us, length us, event | category | flops | bytes accessed | tf_op | source)
XLA Modules:
  0.0 94.0 jit_solution(3389358505474004286)
XLA Ops:
  0.6 90.8 %expert_layer.1 = (bf16[16,2048]{1,0:T(8,128)(2,1)}, bf16[16,2048]{1,0:T(8,128)(2,1)}, f32[2,16]{1,0:T(2,128)}, bf16[192,2048]{1,0:T(8,128)(2,1)}, bf16[192,2048]{1,0:T(8,128)(2,1)}, /*index=5*/bf16[192,2048]{1,0:T(8,128)(2,1)}) custom-call(bf16[128,256]{1,0:T(8,128)(2,1)} %h_hbm.1, bf16[128,256]{1,0:T(8,128)(2,1)} %g_hbm.1, s32[2,128]{1,0:T(2,128)} %bitcast.14, ...), custom_call_target="tpu_custom_call" | custom-call | tf_op jit(solution)/shard_map/expert_layer/pallas_call | solution.py:571
  91.4 2.6 %results.1 = (bf16[16,2048]{1,0:T(8,128)(2,1)}, bf16[16,2048]{1,0:T(8,128)(2,1)}, f32[2,16]{1,0:T(2,128)}, bf16[192,2048]{1,0:T(8,128)(2,1)}, bf16[192,2048]{1,0:T(8,128)(2,1)}, /*index=5*/bf16[192,2048]{1,0:T(8,128)(2,1)}) custom-call(bf16[16,2048]{1,0:T(8,128)(2,1)} %get-tuple-element.18.refs_0_, bf16[16,2048]{1,0:T(8,128)(2,1)} %get-tuple-element.19.refs_1_, ...), custom_call_target="tpu_custom_call" | custom-call | tf_op jit(solution)/shard_map/results/pallas_call | solution.py:584

commit v5 on v4

--- a/solution.py
+++ b/solution.py
@@ -49,10 +49,10 @@
 
 
 def kernel(
-    h_hbm, g_hbm, ids_ref, wrow_ref, gain_ref, wg_hbm, wu_hbm, wd_hbm,
+    h_hbm, g_hbm, ids_hbm, wrow_hbm, gain_hbm, wg_hbm, wu_hbm, wd_hbm,
     lo_ref, ig_ref, rg_ref, gu_out, uu_out, du_out,
     wg, wu, wd, gu, uu, du,
-    tok, meta, hx, zout, zin, gat, nrm, par, got, fout, fback, loc, fifth_in, picked, fin, fin_in,
+    ids_ref, wrow_ref, gain_ref, spreads, tok, meta, hx, zout, zin, gat, nrm, par, got, fout, fback, loc, fifth_in, picked, fin, fin_in,
     hid, ggr, ugr, ht, ggt, ugt,
     w_sem, o_sem, own_sem, meta_send, meta_recv, tok_send, tok_recv, hx_send, hx_recv,
     z_send, z_recv, c_send, c_recv, e_send, e_recv, f_send, f_recv, l_send, l_recv, y_send, y_recv,
@@ -95,6 +95,11 @@
     def wait(ref, sem):
         pltpu.make_async_copy(ref, ref, sem).wait()
 
+    routes = [
+        pltpu.make_async_copy(ids_hbm, ids_ref, own_sem.at[2]),
+        pltpu.make_async_copy(wrow_hbm, wrow_ref, own_sem.at[3]),
+        pltpu.make_async_copy(gain_hbm, gain_ref, own_sem.at[4]),
+    ]
     own = [
         pltpu.make_async_copy(h_hbm, tok.at[0, :, 0:WIDTH], own_sem.at[0]),
         pltpu.make_async_copy(g_hbm, tok.at[0, :, WIDTH : 2 * WIDTH], own_sem.at[1]),
@@ -104,20 +109,20 @@
         pltpu.make_async_copy(wu_hbm, wu, w_sem.at[1]),
         pltpu.make_async_copy(wd_hbm, wd, w_sem.at[2]),
     ]
-    for copy in own + weights:
+    for copy in routes + own + weights:
         copy.start()
 
     barrier = pltpu.get_barrier_semaphore()
 
-    def greet(i, carry):
-        off = 1 + lax.rem(i + 20, NZ * NJ - 1)
-        pl.semaphore_signal(barrier, inc=1, device_id=here + lax.rem(exp + off, NZ * NJ), device_id_type=LOGICAL)
-        return carry
-
-    lax.fori_loop(0, NZ * NJ - 1, greet, 0)
+    for off in sorted(range(NZ), key=lambda off: -min(off, NZ - off)):
+        for d in range(NJ):
+            if off or d:
+                pl.semaphore_signal(barrier, inc=1, device_id=at_place(off, d), device_id_type=LOGICAL)
     for ro in range(1, reps):
         pl.semaphore_signal(barrier, inc=1, device_id=at(ro // 2, ro % 2), device_id_type=LOGICAL)
 
+    for copy in routes:
+        copy.wait()
     ids = ids_ref[...]
     expert_rows = iota((NZ * NJ, 128), 0)
     hits = [(expert_rows == ids[k : k + 1, :]).astype(F32) for k in range(2)]
@@ -152,6 +157,9 @@
         zout[c] = jnp.where(part_of >= 2, weight * tiles, tiles).astype(BF16)
 
     build(MAIN[0])
+    row, col = iota((ROWS, 4 * ROWS), 0), iota((ROWS, 4 * ROWS), 1)
+    for part in range(4):
+        spreads[part] = (col == 16 * (row >> 2) + 4 * part + (row & 3)).astype(F32).astype(BF16)
     pl.semaphore_wait(barrier, NZ * NJ - 1 + reps - 1)
 
     def send_tiles(src, dst, ssem, rsem, c, sign):
@@ -195,9 +203,10 @@
         send(tok.at[2], tok.at[3], tok_send, tok_recv.at[2], at_place(0, 1))
 
     def spread(part, to_blocks):
+        if not to_blocks:
+            return spreads[part]
         r, t = iota((ROWS, 4 * ROWS), 0), iota((ROWS, 4 * ROWS), 1)
-        tile, d = (r & 15, r >> 4) if to_blocks else (r >> 2, r & 3)
-        return (t == 16 * tile + 4 * part + d).astype(F32).astype(BF16)
+        return (t == 16 * (r & 15) + 4 * part + (r >> 4)).astype(F32).astype(BF16)
 
     def to_tiles(rows):
         tiles = None
@@ -396,9 +405,9 @@
     stages = (
         (9, stage_7), (6, stage_6), (5, stage_5), (4, stage_4), (3, stage_3), (2, stage_2), (1, stage_1), (0, stage_0)
     )
-    first_free = CHUNKS + 3
+    first_free = CHUNKS + 6
     ticks = CHUNKS + stages[0][0]
-    per_tick = 2
+    per_tick = reps // 2
 
     def tick(t, carry):
         for lag, stage in reversed(stages):
@@ -418,17 +427,6 @@
     picked[...] = jnp.zeros_like(picked)
     hand_on()
     send_fifth_rows()
-    lax.fori_loop(0, ticks, tick, 0)
-
-    updates = [
-        pltpu.make_async_copy(gu, gu_out, o_sem.at[0]),
-        pltpu.make_async_copy(uu, uu_out, o_sem.at[1]),
-        pltpu.make_async_copy(du, du_out, o_sem.at[2]),
-    ]
-    for copy in updates:
-        copy.start()
-
-    grad = tok[0, :, WIDTH:].astype(F32)
     diagonal = iota((128, 128), 0) == iota((128, 128), 1)
     w = [jnp.sum(jnp.where(diagonal, meta[0, 2 + k : 3 + k, :], 0.0), axis=1, keepdims=True) for k in range(2)]
     wait(hx.at[pl.ds(0, reps - 1)], hx_recv)
@@ -438,6 +436,17 @@
         part = jnp.sum(v * v, axis=1, keepdims=True)
         squares = part if s == 0 else squares + part
     root = jnp.sqrt(squares / features + EPSILON)
+    lax.fori_loop(0, ticks, tick, 0)
+
+    updates = [
+        pltpu.make_async_copy(gu, gu_out, o_sem.at[0]),
+        pltpu.make_async_copy(uu, uu_out, o_sem.at[1]),
+        pltpu.make_async_copy(du, du_out, o_sem.at[2]),
+    ]
+    for copy in updates:
+        copy.start()
+
+    grad = tok[0, :, WIDTH:].astype(F32)
 
     r = iota((ROWS, 1), 0)
     code = code_of(choose(r & 15, ALL), r >> 4, jnp.full_like(r, 4))
@@ -531,6 +540,10 @@
     dma = pltpu.SemaphoreType.DMA
     rows = CHUNKS * ROWS
     scratch = [matrix] * 6 + [
+        pltpu.VMEM((2, tokens), jnp.int32),
+        pltpu.VMEM((2, tokens), F32),
+        pltpu.VMEM((1, features), F32),
+        pltpu.VMEM((4, ROWS, 4 * ROWS), BF16),
         pltpu.VMEM((NJ, tokens, 2 * WIDTH), BF16),
         pltpu.VMEM((NJ, 8, tokens), F32),
         pltpu.VMEM((reps, share, WIDTH), BF16),
@@ -551,7 +564,7 @@
     scratch += [pltpu.VMEM((CHUNKS, ROWS, units), BF16)] * 3
     scratch += [pltpu.VMEM((units, rows), BF16)] * 3
     scratch += [
-        dma((3,)), dma((3,)), dma((2,)),
+        dma((3,)), dma((3,)), dma((5,)),
         dma, dma, dma, dma((3,)),
         dma, dma,
         dma((CHUNKS,)), dma((CHUNKS,)),
@@ -571,7 +584,7 @@
     outs = pl.pallas_call(
         kernel,
         out_shape=kinds,
-        in_specs=[hbm] * 2 + [vmem] * 3 + [hbm] * 3,
+        in_specs=[hbm] * 8,
         out_specs=(vmem, vmem, vmem, anywhere, anywhere, anywhere),
         scratch_shapes=scratch,
         compiler_params=pltpu.CompilerParams(

time: 94.2 us -> 92.3 us (0.980)
  Pallas kernels: 93.4 us -> 91.5 us
    pallas_call x1, Pallas kernels: 90.8 us -> 88.9 us  [body(): pl.pallas_call(kernel, out_shape=kinds, in_specs=[hbm] * 8, out_specs=(vm...]
where the time goes in v5:
time: 92.3 us; the launch traced here: 92.1 us
  Pallas kernels  91.5 us (99%)
    pallas_call x1, Pallas kernels, body(): pl.pallas_call(kernel, out_shape=kinds, in_specs=[hbm] * 8, out_specs=(vm...  88.9 us
    pallas_call x1, Pallas kernels, body(): pl.pallas_call(hand_out, out_shape=kinds, in_specs=[anywhere] * 6, out_sp...  2.58 us

profile of v5, /device:TPU:1, one launch (start us, length us, event | category | flops | bytes accessed | tf_op | source)
XLA Modules:
  0.0 92.1 jit_solution(6140028694235520132)
XLA Ops:
  0.6 88.9 %expert_layer.1 = (bf16[16,2048]{1,0:T(8,128)(2,1)}, bf16[16,2048]{1,0:T(8,128)(2,1)}, f32[2,16]{1,0:T(2,128)}, bf16[192,2048]{1,0:T(8,128)(2,1)}, bf16[192,2048]{1,0:T(8,128)(2,1)}, /*index=5*/bf16[192,2048]{1,0:T(8,128)(2,1)}) custom-call(bf16[128,256]{1,0:T(8,128)(2,1)} %h_hbm.1, bf16[128,256]{1,0:T(8,128)(2,1)} %g_hbm.1, s32[2,128]{1,0:T(2,128)} %bitcast.14, ...), custom_call_target="tpu_custom_call" | custom-call | tf_op jit(solution)/shard_map/expert_layer/pallas_call | solution.py:584
  89.5 2.6 %results.1 = (bf16[16,2048]{1,0:T(8,128)(2,1)}, bf16[16,2048]{1,0:T(8,128)(2,1)}, f32[2,16]{1,0:T(2,128)}, bf16[192,2048]{1,0:T(8,128)(2,1)}, bf16[192,2048]{1,0:T(8,128)(2,1)}, /*index=5*/bf16[192,2048]{1,0:T(8,128)(2,1)}) custom-call(bf16[16,2048]{1,0:T(8,128)(2,1)} %get-tuple-element.18.refs_0_, bf16[16,2048]{1,0:T(8,128)(2,1)} %get-tuple-element.19.refs_1_, ...), custom_call_target="tpu_custom_call" | custom-call | tf_op jit(solution)/shard_map/results/pallas_call | solution.py:597

commit v6 on v5

--- a/solution.py
+++ b/solution.py
@@ -403,7 +403,7 @@
         du[:, cols] = dot(ht[...], rows_g, (1, 0)).astype(BF16)
 
     stages = (
-        (9, stage_7), (6, stage_6), (5, stage_5), (4, stage_4), (3, stage_3), (2, stage_2), (1, stage_1), (0, stage_0)
+        (8, stage_7), (6, stage_6), (5, stage_5), (4, stage_4), (3, stage_3), (2, stage_2), (1, stage_1), (0, stage_0)
     )
     first_free = CHUNKS + 6
     ticks = CHUNKS + stages[0][0]
@@ -455,6 +455,16 @@
     out_rows = [picked[k, :, 0:WIDTH] for k in range(2)]
     share_out = (w[0] * out_rows[0] + w[1] * out_rows[1]).astype(BF16)
     share_in = (picked[0, :, WIDTH:] + picked[1, :, WIDTH:]).astype(BF16)
+    def share_out_rows(parts, first):
+        rows = slice(share * first, share * (first + len(parts)))
+        for s in range(reps):
+            for i, part in enumerate(parts):
+                fin[s, share * (first + i) : share * (first + i + 1), :] = part[share * s : share * s + share, :]
+        for ro in range(1, reps):
+            to = fin.at[rid(ro // 2, ro % 2), rows, :]
+            send(to, fin_in.at[rep, rows, :], y_send, y_recv, at(ro // 2, ro % 2))
+
+    share_out_rows([share_out[:, 0:128], share_out[:, 128:], share_in[:, 0:128], share_in[:, 128:]], 0)
     dots = [jnp.sum(p * grad, axis=1, keepdims=True) for p in out_rows]
     heads = [d.astype(BF16).astype(F32) for d in dots]
     lane = iota((128, 128), 1)
@@ -462,12 +472,7 @@
         lane == 0, heads[0],
         jnp.where(lane == 1, heads[1], jnp.where(lane == 2, dots[0] - heads[0], jnp.where(lane == 3, dots[1] - heads[1], 0.0))),
     ).astype(BF16)
-    halves = [share_out[:, 0:128], share_out[:, 128:], share_in[:, 0:128], share_in[:, 128:], products]
-    for s in range(reps):
-        for i, half in enumerate(halves):
-            fin[s, share * i : share * i + share, :] = half[share * s : share * s + share, :]
-    for ro in range(1, reps):
-        send(fin.at[rid(ro // 2, ro % 2)], fin_in.at[rep], y_send, y_recv, at(ro // 2, ro % 2))
+    share_out_rows([products], 4)
     fin_in[rep] = fin[rep]
 
     wait(fin_in.at[pl.ds(0, reps - 1)], y_recv)

time: 92.3 us -> 93.6 us (1.014)
  Pallas kernels: 91.5 us -> 92.8 us
    pallas_call x1, Pallas kernels: 88.9 us -> 90.2 us  [body(): pl.pallas_call(kernel, out_shape=kinds, in_specs=[hbm] * 8, out_specs=(vm...]
where the time goes in v6:
time: 93.6 us; the launch traced here: 93.5 us
  Pallas kernels  92.8 us (99%)
    pallas_call x1, Pallas kernels, body(): pl.pallas_call(kernel, out_shape=kinds, in_specs=[hbm] * 8, out_specs=(vm...  90.2 us
    pallas_call x1, Pallas kernels, body(): pl.pallas_call(hand_out, out_shape=kinds, in_specs=[anywhere] * 6, out_sp...  2.58 us

profile of v6, /device:TPU:1, one launch (start us, length us, event | category | flops | bytes accessed | tf_op | source)
XLA Modules:
  0.0 93.5 jit_solution(11824464931189131175)
XLA Ops:
  0.6 90.2 %expert_layer.1 = (bf16[16,2048]{1,0:T(8,128)(2,1)}, bf16[16,2048]{1,0:T(8,128)(2,1)}, f32[2,16]{1,0:T(2,128)}, bf16[192,2048]{1,0:T(8,128)(2,1)}, bf16[192,2048]{1,0:T(8,128)(2,1)}, /*index=5*/bf16[192,2048]{1,0:T(8,128)(2,1)}) custom-call(bf16[128,256]{1,0:T(8,128)(2,1)} %h_hbm.1, bf16[128,256]{1,0:T(8,128)(2,1)} %g_hbm.1, s32[2,128]{1,0:T(2,128)} %bitcast.14, ...), custom_call_target="tpu_custom_call" | custom-call | tf_op jit(solution)/shard_map/expert_layer/pallas_call | solution.py:589
  90.9 2.6 %results.1 = (bf16[16,2048]{1,0:T(8,128)(2,1)}, bf16[16,2048]{1,0:T(8,128)(2,1)}, f32[2,16]{1,0:T(2,128)}, bf16[192,2048]{1,0:T(8,128)(2,1)}, bf16[192,2048]{1,0:T(8,128)(2,1)}, /*index=5*/bf16[192,2048]{1,0:T(8,128)(2,1)}) custom-call(bf16[16,2048]{1,0:T(8,128)(2,1)} %get-tuple-element.18.refs_0_, bf16[16,2048]{1,0:T(8,128)(2,1)} %get-tuple-element.19.refs_1_, ...), custom_call_target="tpu_custom_call" | custom-call | tf_op jit(solution)/shard_map/results/pallas_call | solution.py:602
